TPU v7x, 32 devices: a whole 2x2x4 slice. The times are simulated.
32 devices in a mesh: wide: 8 (over y, x, core), narrow: 4 (over z).
Axes of the slice: x: 2, y: 2, z: 4, core: 2. Of those that a mesh axis runs over, the one named last changes fastest.
Arguments:
- layer_input: bfloat16 [16384, 1024], P(('wide', 'narrow')), may hold values from -6 to 6
- out_grad: bfloat16 [16384, 1024], P(('wide', 'narrow')), may hold values from -6 to 6
- norm_attn_gain: bfloat16 [1024], replicated, may hold values from 0.5 to 1.5
- w_query: bfloat16 [1024, 1024], P(None, 'narrow'), may hold values from -0.0234375 to 0.0234375
- w_key: bfloat16 [1024, 1024], P(None, 'narrow'), may hold values from -0.1875 to 0.1875
- w_value: bfloat16 [1024, 1024], P(None, 'narrow'), may hold values from -0.1875 to 0.1875
- w_out: bfloat16 [1024, 1024], P('narrow'), may hold values from -1 to 1
- rel_table: bfloat16 [32, 16], P(None, 'narrow'), may hold values from -4 to 4
- layout_table: bfloat16 [64, 16], P(None, 'narrow'), may hold values from -4 to 4
- norm_ffn_gain: bfloat16 [1024], replicated, may hold values from 0.5 to 1.5
- w_gate: bfloat16 [1024, 2816], P(None, 'narrow'), may hold values from -0.1875 to 0.1875
- w_up: bfloat16 [1024, 2816], P(None, 'narrow'), may hold values from -0.1875 to 0.1875
- down_projection_weight: bfloat16 [2816, 1024], P('narrow'), may hold values from -0.109375 to 0.109375
- page_lengths: int32 [8, 4], P('wide'), may hold values from 1 to 1024, 2048 in all within a row
- key_mask: int32 [16384], P('wide'), may hold values 0 or 1
- rel_bucket: int32 [16384, 2048], P('wide'), may hold values from 0 to 31
- layout_bucket: int32 [16384, 2048], P('wide'), may hold values from 0 to 63
Outputs:
- layer_out: bfloat16 [16384, 1024], P(('wide', 'narrow'))
- in_grad: float32 [16384, 1024], P(('wide', 'narrow'))
- grad_norm_attn: float32 [1024], P(('wide', 'narrow'))
- grad_query: float32 [1024, 1024], P('wide', 'narrow')
- grad_key: float32 [1024, 1024], P('wide', 'narrow')
- grad_value: float32 [1024, 1024], P('wide', 'narrow')
- grad_out_proj: float32 [1024, 1024], P('narrow', 'wide')
- grad_rel_table: float32 [32, 16], P('wide', 'narrow')
- grad_layout_table: float32 [64, 16], P('wide', 'narrow')
- grad_norm_ffn: float32 [1024], P(('wide', 'narrow'))
- grad_gate: float32 [1024, 2816], P('wide', 'narrow')
- grad_up: float32 [1024, 2816], P('wide', 'narrow')
- grad_down: float32 [2816, 1024], P('narrow', 'wide')
Inputs may be any that keep to these rules, and one draw needn't show every extreme that they name: `page_lengths`: each row sums to 2048; the pages fill the block of tokens of that index of wide in order, and one of them has exactly 1024 tokens.
All inputs are finite; a program needn't handle non-finite values. No bound on the sum of `key_mask` on one device may be relied on, other than what follows from the above.
Results may differ from a plain program's by a relative error of at most 0.015.
Values may be sent and summed in bfloat16 or wider, within the bound.
No kernel may reach another device: no remote copies, remote signals or barrier semaphores. Data moves between devices by JAX's collectives and lax.ppermute only.
A program may use at most 320 MiB of HBM per device.

v0:
```python
import functools
import jax
import jax.numpy as jnp
from jax import lax
from jax.experimental import pallas as pl
from jax.experimental.pallas import tpu as pltpu
from jax.sharding import PartitionSpec as P

DH = 64
BIAS_SCALE = 4096.0
LOG2E = 1.4426950408889634
f32 = jnp.float32
bf16 = jnp.bfloat16
NT = (((1,), (1,)), ((), ()))
NN = (((1,), (0,)), ((), ()))


def dot(a, b, dims=NN):
    return lax.dot_general(a, b, dims, preferred_element_type=f32)


def key_window(len_ref, first, last, count, width):
    ends = []
    total = 0
    for p in range(len_ref.shape[1]):
        total = total + len_ref[0, p]
        ends.append(total)
    start = 0
    stop = count
    for e in ends:
        start = jnp.where(e <= first, e, start)
    for e in reversed(ends):
        stop = jnp.where(e > last, e, stop)
    base = (start // 128) * 128
    steps = (stop - base + width - 1) // width
    base = jnp.minimum(base, count - steps * width)
    return ends, base, steps


def for_chunks(base, steps, width, group, body):
    def many(j, carry):
        body(pl.multiple_of(base + j * (group * width), 128), group * width)
        return carry

    def single(j, carry):
        body(pl.multiple_of(base + j * width, 128), width)
        return carry

    if group > 1:
        lax.fori_loop(0, steps // group, many, 0)
    lax.fori_loop((steps // group) * group if group > 1 else 0, steps, single, 0)


def own_half(shape, head):
    lane = lax.broadcasted_iota(jnp.int32, shape, len(shape) - 1)
    return (lane < DH) if head % 2 == 0 else (lane >= DH)


def fill_values(vext, v_ref, heads):
    for h in range(heads):
        vp = v_ref[:, (h // 2) * 128:(h // 2 + 1) * 128]
        vext[h] = jnp.where(own_half(vp.shape, h), vp, jnp.ones_like(vp))


def half_norms(rows):
    lane = lax.broadcasted_iota(jnp.int32, (128, 128), 0)
    column = lax.broadcasted_iota(jnp.int32, (128, 128), 1)
    same = ((lane < DH) == (column < DH)).astype(bf16)
    squares = (rows.astype(f32) * rows.astype(f32)).astype(bf16)
    return jnp.max(dot(squares, same)) * f32(1.02)


HIDDEN_PAIR = -(1 << 31)


def pair_bias_kernel(len_ref, rel_ref, lay_ref, tab_ref, kmask_ref, word_ref, code_ref, colcode, *, width, group):
    tq, count = rel_ref.shape
    pairs = word_ref.shape[0]
    i = pl.program_id(0)
    t0 = i * tq
    ends, base, steps = key_window(len_ref, t0, t0 + tq - 1, count, width)

    @pl.when(i == 0)
    def _():
        pos = lax.broadcasted_iota(jnp.int32, (8, count), 1)
        page = jnp.zeros((8, count), jnp.int32)
        for e in ends:
            page = page + (pos >= e).astype(jnp.int32)
        colcode[...] = jnp.where(kmask_ref[...] == 1, page, -1)

    rowpos = lax.broadcasted_iota(jnp.int32, (tq, 128), 0) + t0
    rowpage = jnp.zeros((tq, 128), jnp.int32)
    for e in ends:
        rowpage = rowpage + (rowpos >= e).astype(jnp.int32)
    lanes = lax.broadcasted_iota(jnp.int32, (tq, 128), 1)
    tabs = [jnp.broadcast_to(tab_ref[n:n + 1, :], (tq, 128)) for n in range(2 * pairs)]

    def chunk(c0, size):
        for half in range(size // 128):
            cc = pl.multiple_of(c0 + half * 128, 128)
            here = pl.ds(cc, 128)
            rel = rel_ref[:, here]
            lay = lay_ref[:, here]
            code_ref[:, here] = (rel + lay * 32).astype(jnp.int16)
            col = jnp.broadcast_to(colcode[0:1, here], (tq, 128))
            seen = (rowpage == col) | (rowpos == lanes + cc)
            for p in range(pairs):
                word = (jnp.take_along_axis(tabs[2 * p], rel, axis=1, mode="promise_in_bounds")
                        + jnp.take_along_axis(tabs[2 * p + 1], lay, axis=1, mode="promise_in_bounds"))
                word_ref[p, :, here] = jnp.where(seen, word, HIDDEN_PAIR)

    for_chunks(base, steps, width, group, chunk)


def pair_bias(page_lengths, rel, lay, tab, kmask, tq=256, width=256, group=2):
    count = rel.shape[0]
    pairs = tab.shape[0] // 2
    tile = lambda i: (i, 0)
    return pl.pallas_call(
        functools.partial(pair_bias_kernel, width=width, group=group),
        grid=(count // tq,),
        in_specs=[
            pl.BlockSpec(memory_space=pltpu.SMEM),
            pl.BlockSpec((tq, count), tile),
            pl.BlockSpec((tq, count), tile),
            pl.BlockSpec(tab.shape, lambda i: (0, 0)),
            pl.BlockSpec((1, count), lambda i: (0, 0)),
        ],
        out_specs=[
            pl.BlockSpec((pairs, tq, count), lambda i: (0, i, 0)),
            pl.BlockSpec((tq, count), tile),
        ],
        out_shape=[
            jax.ShapeDtypeStruct((pairs, count, count), jnp.int32),
            jax.ShapeDtypeStruct((count, count), jnp.int16),
        ],
        scratch_shapes=[pltpu.VMEM((8, count), jnp.int32)],
        compiler_params=pltpu.CompilerParams(vmem_limit_bytes=56 << 20),
        cost_estimate=pl.CostEstimate(flops=count * count * 1024, bytes_accessed=120 << 20, transcendentals=0),
        name="pair_bias",
    )(page_lengths, rel, lay, tab, kmask.reshape(1, count))


def forward_kernel(len_ref, q_ref, k_ref, v_ref, word_ref, att_ref, rinv_ref, e_ref,
                   s_scr, m_scr, acc_scr, vext, knorm, *, width, group):
    tq, count = word_ref.shape[1:]
    heads, pairs = 2, 1
    i = pl.program_id(0)
    t0 = i * tq
    ends, base, steps = key_window(len_ref, t0, t0 + tq - 1, count, width)

    @pl.when(i == 0)
    def _():
        fill_values(vext, v_ref, heads)
        for p in range(pairs):
            knorm[p] = half_norms(k_ref[:, p * 128:(p + 1) * 128])

    scaled = []
    largest = f32(0.0)
    for h in range(heads):
        qp = q_ref[:, (h // 2) * 128:(h // 2 + 1) * 128]
        scaled.append(jnp.where(own_half(qp.shape, h), qp * bf16(BIAS_SCALE), jnp.zeros_like(qp)))
        if h % 2 == 0:
            largest = jnp.maximum(largest, half_norms(qp) * knorm[h // 2])
    def scores(c0, width, use):
        raw = [dot(scaled[h], k_ref[pl.ds(c0, width), (h // 2) * 128:(h // 2 + 1) * 128], NT)
               for h in range(heads)]
        for half in range(width // 128):
            cc = pl.multiple_of(c0 + half * 128, 128)
            word = word_ref[0, :, pl.ds(cc, 128)]
            hidden = word == HIDDEN_PAIR
            parts = ((word & 0xFFFF).astype(f32), (word >> 16).astype(f32))
            for h in range(heads):
                bias = jnp.where(hidden, f32(-1e30), parts[h])
                use(h, half, cc, raw[h][:, half * 128:(half + 1) * 128] + bias)

    for h in range(heads):
        acc_scr[h] = jnp.zeros((tq, 128), f32)
    bounded = jnp.sqrt(largest) + 8.0 <= 60.0

    @pl.when(bounded)
    def _():
        def chunk(c0, size):
            pieces = {}

            def use(h, half, cc, s):
                e = jnp.exp2(s * f32(LOG2E / BIAS_SCALE)).astype(bf16)
                e_ref[h, :, pl.ds(cc, 128)] = e
                pieces[h, half] = e

            scores(c0, size, use)
            for h in range(heads):
                e = jnp.concatenate([pieces[h, half] for half in range(size // 128)], axis=1)
                acc_scr[h] += dot(e, vext[h, pl.ds(c0, size), :])

        for_chunks(base, steps, width, group, chunk)

    @pl.when(jnp.logical_not(bounded))
    def _():
        for h in range(heads):
            m_scr[h] = jnp.full((tq, 128), -3e38, f32)

        def first(j, carry):
            def use(h, half, cc, s):
                s_scr[h, :, pl.ds(cc, 128)] = s
                m_scr[h] = jnp.maximum(m_scr[h], s)

            scores(pl.multiple_of(base + j * width, 128), width, use)
            return carry

        lax.fori_loop(0, steps, first, 0)
        for h in range(heads):
            top = jnp.max(m_scr[h], axis=1, keepdims=True)

            def second(j, carry):
                c0 = pl.multiple_of(base + j * width, 128)
                e = jnp.exp2((s_scr[h, :, pl.ds(c0, width)] - top) * f32(LOG2E / BIAS_SCALE)).astype(bf16)
                e_ref[h, :, pl.ds(c0, width)] = e
                acc_scr[h] += dot(e, vext[h, pl.ds(c0, width), :])
                return carry

            lax.fori_loop(0, steps, second, 0)

    low = own_half((tq, 128), 0)
    for p in range(pairs):
        even, odd = acc_scr[2 * p], acc_scr[2 * p + 1]
        rinv = 1.0 / pltpu.roll(jnp.where(low, odd, even), DH, 1)
        att_ref[:, p * 128:(p + 1) * 128] = (jnp.where(low, even, odd) * rinv).astype(bf16)
        rinv_ref[:, p * 128:(p + 1) * 128] = rinv


def attention_forward(page_lengths, proj, words, pair, tq=256, width=256, group=2):
    count = proj.shape[0]
    pairs = proj.shape[1] // (3 * 128)
    tile = lambda i: (i, 0)
    return pl.pallas_call(
        functools.partial(forward_kernel, width=width, group=group),
        grid=(count // tq,),
        in_specs=[
            pl.BlockSpec(memory_space=pltpu.SMEM),
            pl.BlockSpec((tq, 128), lambda i: (i, pair)),
            pl.BlockSpec((count, 128), lambda i: (0, pairs + pair)),
            pl.BlockSpec((count, 128), lambda i: (0, 2 * pairs + pair)),
            pl.BlockSpec((1, tq, count), lambda i: (pair, i, 0)),
        ],
        out_specs=[
            pl.BlockSpec((tq, 128), tile),
            pl.BlockSpec((tq, 128), tile),
            pl.BlockSpec((2, tq, count), lambda i: (0, i, 0)),
        ],
        out_shape=[
            jax.ShapeDtypeStruct((count, 128), bf16),
            jax.ShapeDtypeStruct((count, 128), f32),
            jax.ShapeDtypeStruct((2, count, count), bf16),
        ],
        scratch_shapes=[
            pltpu.VMEM((2, tq, count), f32),
            pltpu.VMEM((2, tq, 128), f32),
            pltpu.VMEM((2, tq, 128), f32),
            pltpu.VMEM((2, count, 128), bf16),
            pltpu.SMEM((1,), f32),
        ],
        compiler_params=pltpu.CompilerParams(vmem_limit_bytes=56 << 20),
        cost_estimate=pl.CostEstimate(
            flops=count * count * 512, bytes_accessed=80 << 20, transcendentals=count * count),
        name="attention_forward",
    )(page_lengths, proj, proj, proj, words)


def bias_words(rel_table, layout_table):
    def pack(table):
        whole = jnp.round(table.astype(f32) * BIAS_SCALE).astype(jnp.int32)
        low = jnp.clip(whole[:, 0::2] + 16384, 0, 32767)
        high = jnp.clip(whole[:, 1::2], -16383, 16383)
        words = (high * 65536 + low).T
        return jnp.pad(words, ((0, 0), (0, 128 - words.shape[1])))
    both = jnp.stack([pack(rel_table), pack(layout_table)], axis=1)
    return both.reshape(-1, 128)


def signs(code, shift, bits):
    return [jnp.where((code & jnp.int16(1 << (shift + b))) == 0, bf16(1.0), bf16(-1.0))
            for b in range(bits)]


def walsh(sign_list):
    out = [None]
    for s in sign_list:
        out = out + [s if o is None else o * s for o in out]
    return out


def backward_kernel(len_ref, q_ref, k_ref, v_ref, da_ref, *refs, width, heads, group):
    tq = q_ref.shape[0]
    count = k_ref.shape[0]
    pairs = heads // 2
    e_refs, att_refs, rinv_refs = refs[:pairs], refs[pairs:2 * pairs], refs[2 * pairs:3 * pairs]
    dp_ref, ds_ref = refs[3 * pairs:3 * pairs + 2]
    vext, lhs_scr, dat_scr, qt_scr, dq_scr, dkt, dvt = refs[3 * pairs + 2:]
    i = pl.program_id(0)
    t0 = i * tq
    ends, base, steps = key_window(len_ref, t0, t0 + tq - 1, count, width)

    @pl.when(i == 0)
    def _():
        fill_values(vext, v_ref, heads)
        dkt[...] = jnp.zeros_like(dkt)
        dvt[...] = jnp.zeros_like(dvt)

    low = own_half((tq, 128), 0)
    lane = lax.broadcasted_iota(jnp.int32, (tq, 128), 1)
    first_part = (lane & 32) == 0
    for p in range(pairs):
        cols = slice(p * 128, (p + 1) * 128)
        da = (da_ref[:, cols].astype(f32) * rinv_refs[p][...]).astype(bf16)
        daf = da.astype(f32)
        prod = daf * att_refs[p][...].astype(f32)
        for r in range(2):
            own = low if r == 0 else jnp.logical_not(low)
            delta = jnp.sum(jnp.where(own, prod, 0.0), axis=1, keepdims=True) * f32(-1.0 / 32)
            high = delta.astype(bf16).astype(f32)
            rest = delta - high
            lhs_scr[2 * p + r] = jnp.where(own, daf, jnp.where(first_part, high, rest)).astype(bf16)
        dat_scr[p] = daf.T.astype(bf16)
        qt_scr[p] = q_ref[:, cols].astype(f32).T.astype(bf16)
        dq_scr[p] = jnp.zeros((tq, 128), f32)

    def chunk(c0, size):
        here = pl.ds(c0, size)
        for p in range(pairs):
            kp = k_ref[here, p * 128:(p + 1) * 128]
            dqs = []
            for r in range(2):
                h = 2 * p + r
                rows = slice(r * DH, (r + 1) * DH)
                e = e_refs[p][r, :, here]
                d = dot(lhs_scr[h], vext[h, here, :], NT)
                ds = (e.astype(f32) * d).astype(bf16)
                ds_ref[h, :, here] = ds
                dqs.append(dot(ds, kp))
                dkt[p, rows, here] += dot(qt_scr[p, rows, :], ds)
                dvt[p, rows, here] += dot(dat_scr[p, rows, :], e)
            dq_scr[p] += jnp.where(low, dqs[0], dqs[1])

    for_chunks(base, steps, width, group, chunk)
    for p in range(pairs):
        dp_ref[pl.ds(pl.multiple_of(t0, tq), tq), p * 128:(p + 1) * 128] = dq_scr[p].astype(bf16)

    @pl.when(i == pl.num_programs(0) - 1)
    def _():
        for n, grads in enumerate((dkt, dvt)):
            for p in range(pairs):
                at = ((n + 1) * pairs + p) * 128
                for c in range(0, count, 256):
                    dp_ref[c:c + 256, at:at + 128] = grads[p, :, c:c + 256].T.astype(bf16)


def attention_backward(page_lengths, proj, exps, d_att, atts, rinvs, tq=256, width=256, group=2):
    count = proj.shape[0]
    hc = proj.shape[1] // 3
    heads = hc // DH
    pairs = heads // 2
    grid = (count // tq,)
    tile = lambda i: (i, 0)
    fixed = lambda i: (0, 0)
    return pl.pallas_call(
        functools.partial(backward_kernel, width=width, heads=heads, group=group),
        grid=grid,
        in_specs=[
            pl.BlockSpec(memory_space=pltpu.SMEM),
            pl.BlockSpec((tq, hc), tile),
            pl.BlockSpec((count, hc), lambda i: (0, 1)),
            pl.BlockSpec((count, hc), lambda i: (0, 2)),
            pl.BlockSpec((tq, hc), tile),
        ] + [pl.BlockSpec((2, tq, count), lambda i: (0, i, 0))] * pairs + [pl.BlockSpec((tq, 128), tile)] * (2 * pairs),
        out_specs=[
            pl.BlockSpec((count, 3 * hc), fixed),
            pl.BlockSpec((heads, tq, count), lambda i: (0, i, 0)),
        ],
        out_shape=[
            jax.ShapeDtypeStruct((count, 3 * hc), bf16),
            jax.ShapeDtypeStruct((heads, count, count), bf16),
        ],
        scratch_shapes=[
            pltpu.VMEM((heads, count, 128), bf16),
            pltpu.VMEM((heads, tq, 128), bf16),
            pltpu.VMEM((pairs, 128, tq), bf16),
            pltpu.VMEM((pairs, 128, tq), bf16),
            pltpu.VMEM((pairs, tq, 128), f32),
            pltpu.VMEM((pairs, 128, count), f32),
            pltpu.VMEM((pairs, 128, count), f32),
        ],
        compiler_params=pltpu.CompilerParams(vmem_limit_bytes=56 << 20),
        cost_estimate=pl.CostEstimate(
            flops=heads * count * count * 512, bytes_accessed=150 << 20, transcendentals=0),
        name="attention_backward",
    )(page_lengths, proj, proj, proj, d_att, *exps, *atts, *rinvs)


def table_kernel(len_ref, ds_ref, code_ref, hl_ref, hr_ref, *bufs, width, parts):
    heads, tq, count = ds_ref.shape
    i = pl.program_id(0)
    t0 = i * tq
    ends, base, steps = key_window(len_ref, t0, t0 + tq - 1, count, width)

    @pl.when(i == 0)
    def _():
        hl_ref[...] = jnp.zeros_like(hl_ref)
        hr_ref[...] = jnp.zeros_like(hr_ref)

    one = jnp.ones((16, width), bf16)

    def chunk(j, carry):
        c0 = pl.multiple_of(base + j * width, 128)
        here = pl.ds(c0, width)
        blocks = tq // 16 // parts
        for part in range(parts):
            left, blay, brel = bufs[3 * part:3 * part + 3]
            for b in range(blocks):
                at = 16 * (part * blocks + b)
                rows = slice(at, at + 16)
                span = slice(b * width, (b + 1) * width)
                code = code_ref[rows, here]
                rel_signs = signs(code, 0, 5)
                lay_signs = signs(code, 5, 6)
                left_lay = walsh(lay_signs[:2])[1:]
                for h in range(heads):
                    ds = ds_ref[h, rows, here]
                    for a, func in enumerate(left_lay + [None, rel_signs[0]]):
                        place = 16 * (a * heads + h)
                        left[place:place + 16, span] = ds if func is None else ds * func
                for n, func in enumerate(walsh(lay_signs[2:])):
                    blay[16 * n:16 * (n + 1), span] = one if func is None else func
                for n, func in enumerate(walsh(rel_signs[1:])):
                    brel[16 * n:16 * (n + 1), span] = one if func is None else func
            hl_ref[...] += dot(left[:64 * heads, :], blay[...], NT)
            hr_ref[...] += dot(left[48 * heads:80 * heads, :], brel[...], NT)
        return carry

    lax.fori_loop(0, steps, chunk, 0)


def table_grads(page_lengths, ds, code, tq=256, width=256, parts=2):
    heads, count, _ = ds.shape
    deep = tq // 16 * width // parts
    fixed = lambda i: (0, 0)
    return pl.pallas_call(
        functools.partial(table_kernel, width=width, parts=parts),
        grid=(count // tq,),
        in_specs=[
            pl.BlockSpec(memory_space=pltpu.SMEM),
            pl.BlockSpec((heads, tq, count), lambda i: (0, i, 0)),
            pl.BlockSpec((tq, count), lambda i: (i, 0)),
        ],
        out_specs=[
            pl.BlockSpec((64 * heads, 256), fixed),
            pl.BlockSpec((32 * heads, 256), fixed),
        ],
        out_shape=[
            jax.ShapeDtypeStruct((64 * heads, 256), f32),
            jax.ShapeDtypeStruct((32 * heads, 256), f32),
        ],
        scratch_shapes=[
            pltpu.VMEM((80 * heads, deep), bf16),
            pltpu.VMEM((256, deep), bf16),
            pltpu.VMEM((256, deep), bf16),
        ] * parts,
        compiler_params=pltpu.CompilerParams(vmem_limit_bytes=56 << 20),
        cost_estimate=pl.CostEstimate(
            flops=heads * count * count * 512, bytes_accessed=150 << 20, transcendentals=0),
        name="table_grads",
    )(page_lengths, ds, code)


def bucket_sums(raw, heads):
    right = raw.shape[1] // 16
    left = raw.shape[0] // (16 * heads)
    cube = raw.reshape(left, heads, 16, right, 16)
    traced = jnp.sum(cube * jnp.eye(16, dtype=f32)[None, None, :, None, :], axis=(2, 4))
    if left == 4:
        traced = jnp.concatenate([traced[3:], traced[:3]], axis=0)

    def table(n):
        v = lax.iota(jnp.int32, n)
        both = v[:, None] & v[None, :]
        return (1 - 2 * (lax.population_count(both) & 1)).astype(f32)

    out = jnp.einsum("ahn,ax,ny->yxh", traced, table(left), table(right), precision=lax.Precision.HIGHEST)
    return out.reshape(left * right, heads) / (left * right)


TANH_SLOPE = 0.7978845608028654
CUBE = 0.044715


def feed_forward_kernel(far, x_ref, g_ref, *refs):
    weights, (hidden_ref, d_gate_ref, d_up_ref, dn_ref) = refs[:-4], refs[-4:]
    units = hidden_ref.shape[1]
    if far:
        step = pad_lanes(units)
        gate_weight, up_weight, down = [weights[0][:, n * step:n * step + units] for n in range(3)]
        ahead, back = NN, NT
    else:
        gate_weight, up_weight, down = [w[...] for w in weights]
        ahead, back = NT, NN
    x = x_ref[...]
    d_hidden = dot(g_ref[...], down, ahead)
    gate = dot(x, gate_weight, ahead)
    up = dot(x, up_weight, ahead)
    square = gate * gate
    t = jnp.tanh(TANH_SLOPE * gate * (1.0 + CUBE * square))
    half = 0.5 + 0.5 * t
    gelu = gate * half
    slope = half + (0.5 * TANH_SLOPE) * gate * (1.0 - t * t) * (1.0 + (3 * CUBE) * square)
    d_gate = (d_hidden * up * slope).astype(bf16)
    d_up = (d_hidden * gelu).astype(bf16)
    hidden_ref[...] = (gelu * up).astype(bf16)
    d_gate_ref[...] = d_gate
    d_up_ref[...] = d_up
    dn_ref[...] = dot(d_gate, gate_weight, back) + dot(d_up, up_weight, back)


def feed_forward(x, g, units, weights, shard=None, tile=256):
    tokens, features = x.shape
    tile = min(tile, tokens)
    rows = lambda n: pl.BlockSpec((tile, n), lambda i: (i, 0))
    if shard is None:
        weight_specs = [pl.BlockSpec(w.shape, lambda i: (0, 0)) for w in weights]
    else:
        weight_specs = [pl.BlockSpec((features, 3 * pad_lanes(units)), lambda i: (0, shard))]
    return pl.pallas_call(
        functools.partial(feed_forward_kernel, shard is not None),
        grid=(tokens // tile,),
        in_specs=[rows(features), rows(features)] + weight_specs,
        out_specs=[rows(units)] * 3 + [rows(features)],
        out_shape=[jax.ShapeDtypeStruct((tokens, units), bf16)] * 3
        + [jax.ShapeDtypeStruct((tokens, features), f32)],
        compiler_params=pltpu.CompilerParams(vmem_limit_bytes=56 << 20),
        cost_estimate=pl.CostEstimate(
            flops=10 * tokens * features * units, bytes_accessed=10 << 20, transcendentals=tokens * units),
        name="feed_forward",
    )(x, g, *weights)


def pad_lanes(n):
    return (n + 127) // 128 * 128


def weight_grads_kernel(n_left, n_right, *refs):
    lefts = refs[:2 * n_left]
    rights = refs[2 * n_left:-1]
    out_ref = refs[-1]
    rows_in = (((0,), (0,)), ((), ()))
    place = 0
    for n, left in enumerate(n_right):
        a, b = rights[2 * n], rights[2 * n + 1]
        size = a.shape[1]
        value = dot(lefts[2 * left][...], a[...], rows_in) + dot(lefts[2 * left + 1][...], b[...], rows_in)
        out_ref[:, place:place + size] = value.astype(bf16)
        if pad_lanes(size) > size:
            out_ref[:, place + size:place + pad_lanes(size)] = jnp.zeros(
                (out_ref.shape[0], pad_lanes(size) - size), bf16)
        place += pad_lanes(size)


def weight_grads(lefts, rights, groups, tile=256):
    features = lefts[0].shape[1]
    columns = sum(pad_lanes(r.shape[1]) for r in rights[::2])
    column = lambda a: pl.BlockSpec((a.shape[0], tile), lambda i: (0, i))
    whole = lambda a: pl.BlockSpec(a.shape, lambda i: (0, 0))
    return pl.pallas_call(
        functools.partial(weight_grads_kernel, len(lefts) // 2, groups),
        grid=(features // tile,),
        in_specs=[column(a) for a in lefts] + [whole(a) for a in rights],
        out_specs=pl.BlockSpec((tile, columns), lambda i: (i, 0)),
        out_shape=jax.ShapeDtypeStruct((features, columns), bf16),
        compiler_params=pltpu.CompilerParams(vmem_limit_bytes=56 << 20),
        cost_estimate=pl.CostEstimate(
            flops=4 * features * columns * lefts[0].shape[0], bytes_accessed=26 << 20, transcendentals=0),
        name="weight_grads",
    )(*lefts, *rights)


epsilon = 1e-06


def contract_rows(left, right):
    return lax.dot_general(
        left, right, (((0,), (0,)), ((), ())), preferred_element_type=jnp.float32
    )


def contract_cols(left, right):
    return lax.dot_general(
        left, right, (((1,), (1,)), ((), ())), preferred_element_type=jnp.float32
    )


def norm_rows(rows, gain):
    scale = lax.rsqrt(jnp.mean(rows * rows, axis=-1, keepdims=True) + epsilon)
    return (scale, (rows * scale * gain).astype(jnp.bfloat16))


def norm_back(d_normed, rows, scale, gain):
    shaped = d_normed * gain
    cubed = scale * scale * scale
    return scale * shaped - rows * cubed * jnp.mean(shaped * rows, axis=-1, keepdims=True)


def along(array, shift, ring):
    return lax.ppermute(array, "narrow", [(i, (i + shift) % ring) for i in range(ring)])


def swap(array, ring):
    return lax.ppermute(array, "narrow", [(i, i ^ 1) for i in range(ring)])


def rows_of(array, index, count):
    return lax.dynamic_slice_in_dim(array, index * count, count, 0)


def on_device(
    wide,
    ring,
    layer_input,
    out_grad,
    norm_attn_gain,
    w_query,
    w_key,
    w_value,
    w_out,
    rel_table,
    layout_table,
    norm_ffn_gain,
    w_gate,
    w_up,
    down_projection_weight,
    page_lengths,
    key_mask,
    rel_bucket,
    layout_bucket,
):
    tokens, width = layer_input.shape
    head_cols = w_query.shape[1]
    heads = head_cols // DH
    units = w_gate.shape[1]
    padded = pad_lanes(units)
    part = width // wide
    me = lax.axis_index("narrow")
    my_wide = lax.axis_index("wide")
    gain_attn = norm_attn_gain.astype(f32)
    gain_ffn = norm_ffn_gain.astype(f32)
    resid = layer_input.astype(f32)

    scale_attn, normed_attn = norm_rows(resid, gain_attn)
    normed_attn_all = lax.all_gather(normed_attn, "narrow", axis=0, tiled=True)

    w_project = jnp.concatenate([w_query, w_key, w_value], axis=1)
    own_rows_gate = rows_of(w_gate, my_wide, part)
    own_rows_up = rows_of(w_up, my_wide, part)
    own_rows_project = rows_of(w_project, my_wide, part)
    down_piece = lax.dynamic_slice_in_dim(down_projection_weight, my_wide * part, part, 1).T
    out_piece = lax.dynamic_slice_in_dim(w_out, my_wide * part, part, 1).T
    ffn_piece = jnp.concatenate(
        [jnp.pad(piece, ((0, 0), (0, padded - units))) for piece in (own_rows_gate, own_rows_up, down_piece)], axis=1)
    out_pieces = [out_piece] + [along(out_piece, d, ring) for d in range(1, ring)]
    words, codes = pair_bias(page_lengths, rel_bucket, layout_bucket, bias_words(rel_table, layout_table), key_mask)
    normed_attn_all, ffn_piece, words = lax.optimization_barrier((normed_attn_all, ffn_piece, words))
    ffn_pieces = [along(ffn_piece, d, ring) for d in range(2, ring, 2)]
    out_t = lax.all_gather(jnp.concatenate(out_pieces, axis=1), "wide", axis=0, tiled=True)

    projected = dot(normed_attn_all, w_project).astype(bf16)
    pairs = head_cols // 128
    first_pair = list(attention_forward(page_lengths, projected, words, 0))
    first_pair[0], ffn_pieces, late_grad = lax.optimization_barrier((first_pair[0], ffn_pieces, out_grad))
    far_pieces = jnp.concatenate(ffn_pieces, axis=1)
    other_grad = swap(late_grad, ring)

    def to_owners(a):
        return [rows_of(a, me, tokens)] + [
            along(rows_of(a, (me + d) % ring, tokens), d, ring) for d in range(1, ring)]

    sent = [to_owners(first_pair[0])]
    results = [first_pair]
    if pairs > 1:
        late_projected, far_pieces = lax.optimization_barrier((projected, far_pieces))
        results += [list(attention_forward(page_lengths, late_projected, words, p)) for p in range(1, pairs)]
    far = lax.all_gather(far_pieces, "wide", axis=0, tiled=True)
    results[-1][0], other_grad, sent[0] = lax.optimization_barrier((results[-1][0], other_grad, sent[0]))
    attended = [r[0] for r in results]
    sent += [to_owners(a) for a in attended[1:]]
    mine = [pieces[d] for d in range(ring) for pieces in sent]
    attended_own = jnp.concatenate(mine, axis=1)
    middle = resid + contract_cols(attended_own, out_t)

    scale_ffn, normed_ffn = norm_rows(middle, gain_ffn)
    other_normed = swap(normed_ffn, ring)
    near = (w_gate.T, w_up.T, down_projection_weight)
    shards = ring // 2
    own = [feed_forward(normed_ffn, out_grad, units, near)]
    own, other_normed, late_project = lax.optimization_barrier((own, other_normed, own_rows_project))
    project_pieces = [along(late_project, d, ring) for d in range(1, ring)]
    other = [feed_forward(other_normed, other_grad, units, near)]
    other += [feed_forward(other_normed, other_grad, units, (far,), s) for s in range(shards - 1)]
    other, project_pieces = lax.optimization_barrier((other, project_pieces))
    w_project_all = lax.all_gather(
        jnp.concatenate([own_rows_project] + project_pieces, axis=1), "wide", axis=0, tiled=True)
    other_d_normed = sum(o[3] for o in other).astype(bf16)
    late_normed, other_d_normed = lax.optimization_barrier((normed_ffn, other_d_normed))
    other_d_normed = swap(other_d_normed, ring)
    own += [feed_forward(late_normed, out_grad, units, (far,), s) for s in range(shards - 1)]
    rights, groups = [], []
    for s in range(shards):
        for n in range(1, 4):
            rights += [own[s][n % 3], other[s][n % 3]]
            groups.append(n // 3)
    sums = weight_grads((normed_ffn, other_normed, out_grad, other_grad), rights, tuple(groups))
    sums, other_d_normed = lax.optimization_barrier((sums, other_d_normed))
    ffn_sums = lax.psum_scatter(sums, "wide", scatter_dimension=0, tiled=True)
    d_normed_ffn = sum(o[3] for o in own) + other_d_normed.astype(f32)
    d_middle = out_grad.astype(f32) + norm_back(d_normed_ffn, middle, scale_ffn, gain_ffn)
    d_middle_low = d_middle.astype(bf16)
    d_attended_own = dot(d_middle_low, out_t).astype(bf16)

    def block(d):
        return d_attended_own[:, d * head_cols : (d + 1) * head_cols]

    d_attended = jnp.zeros((ring * tokens, head_cols), bf16)
    d_attended = lax.dynamic_update_slice_in_dim(d_attended, block(0), me * tokens, 0)
    for d in range(1, ring):
        d_attended = lax.dynamic_update_slice_in_dim(
            d_attended, along(block(d), -d, ring), ((me + d) % ring) * tokens, 0)

    d_middle_late, attended_late, own_hidden, other_hidden = lax.optimization_barrier(
        (d_middle_low, attended_own, [o[0] for o in own], [o[0] for o in other]))
    wout_sums = contract_rows(d_middle_late, attended_late).astype(bf16)
    own_out, other_out = 0.0, 0.0
    for s in range(shards):
        if s == 0:
            down, dims = down_projection_weight, NN
        else:
            at = 3 * padded * (s - 1) + 2 * padded
            down, dims = far[:, at : at + units], NT
        own_out = own_out + dot(own_hidden[s], down, dims)
        other_out = other_out + dot(other_hidden[s], down, dims)
    own_out = own_out + middle
    wout_sums, d_attended, w_project_all, own_out, other_out = lax.optimization_barrier(
        (wout_sums, d_attended, w_project_all, own_out, other_out.astype(bf16)))
    other_out = swap(other_out, ring)

    d_project, d_scores = attention_backward(
        page_lengths, projected, [r[2] for r in results], d_attended, attended, [r[1] for r in results])
    d_project, other_out = lax.optimization_barrier((d_project, other_out))
    leaving = [rows_of(d_project, (me + d) % ring, tokens) for d in range(ring)]
    leaving, d_project, own_out = lax.optimization_barrier((leaving, d_project, own_out))
    mine = leaving[:1] + [along(leaving[d], d, ring) for d in range(1, ring)]
    layer_out = (own_out + other_out.astype(f32)).astype(bf16)
    last_sums = jnp.concatenate([contract_rows(normed_attn_all, d_project).astype(bf16), wout_sums], axis=1)
    last_sums, ffn_sums = lax.optimization_barrier((last_sums, ffn_sums))
    last_sums = lax.psum_scatter(last_sums, "wide", scatter_dimension=0, tiled=True)

    raw_lay, raw_rel = table_grads(page_lengths, d_scores, codes)
    far_sums = [along(ffn_sums[:, 3 * padded * s : 3 * padded * (s + 1)], -2 * s, ring) for s in range(1, shards)]
    raw_lay, raw_rel, mine, far_sums, last_sums = lax.optimization_barrier(
        (raw_lay, raw_rel, mine, far_sums, last_sums))
    grad_relative = bucket_sums(raw_rel, heads)
    grad_layout = bucket_sums(raw_lay, heads)
    tables = jnp.concatenate(
        [grad_relative.reshape(wide, -1, heads), grad_layout.reshape(wide, -1, heads)], axis=1)
    n_rel = grad_relative.shape[0] // wide
    reach = wide // 2
    while reach >= 1:
        bit = (my_wide // reach) % 2
        keep = lax.dynamic_slice_in_dim(tables, bit * reach, reach, 0)
        give = lax.dynamic_slice_in_dim(tables, (1 - bit) * reach, reach, 0)
        tables = keep + lax.ppermute(give, "wide", [(i, i ^ reach) for i in range(wide)])
        reach //= 2
    sum_project = last_sums[:, : 3 * head_cols].astype(f32)
    wout_sums = last_sums[:, 3 * head_cols :]
    far_wout = [along(wout_sums[:, d * head_cols : (d + 1) * head_cols], -d, ring) for d in range(1, ring)]
    sum_tables = tables[0]
    d_project_own = jnp.concatenate(mine, axis=1)
    d_normed_attn = contract_cols(d_project_own, w_project_all)
    in_grad = d_middle + norm_back(d_normed_attn, resid, scale_attn, gain_attn)

    def stripe(shard, n):
        at = padded * (3 * shard + n)
        return ffn_sums[:, at : at + units]

    sum_gate, sum_up, sum_down = [stripe(0, n).astype(f32) for n in range(3)]
    for s in range(1, shards):
        block = far_sums[s - 1].astype(f32)
        sum_gate += block[:, :units]
        sum_up += block[:, padded : padded + units]
        sum_down += block[:, 2 * padded : 2 * padded + units]
    sum_wout = wout_sums[:, :head_cols].astype(f32) + sum(w.astype(f32) for w in far_wout)

    gain_terms = jnp.stack(
        [
            jnp.sum(own_rows_project.astype(f32) * sum_project, axis=1),
            jnp.sum(own_rows_gate.astype(f32) * sum_gate + own_rows_up.astype(f32) * sum_up, axis=1),
        ]
    )
    share = part // ring

    def gain_share(index):
        return lax.dynamic_slice_in_dim(gain_terms, index * share, share, 1)

    gain_sum = gain_share(me)
    for d in range(1, ring):
        gain_sum = gain_sum + along(gain_share((me + d) % ring), d, ring)
    place = my_wide * part + me * share
    gains = lax.dynamic_slice_in_dim(jnp.stack([gain_attn, gain_ffn]), place, share, 1)
    gain_grads = gain_sum / gains
    return (
        layer_out,
        in_grad,
        gain_grads[0],
        sum_project[:, :head_cols],
        sum_project[:, head_cols : 2 * head_cols],
        sum_project[:, 2 * head_cols :],
        sum_wout.T,
        sum_tables[:n_rel],
        sum_tables[n_rel:],
        gain_grads[1],
        sum_gate,
        sum_up,
        sum_down.T,
    )


def solution(mesh):
    placed = (
        P(("wide", "narrow"), None),
        P(("wide", "narrow"), None),
        P(),
        P(None, "narrow"),
        P(None, "narrow"),
        P(None, "narrow"),
        P("narrow", None),
        P(None, "narrow"),
        P(None, "narrow"),
        P(),
        P(None, "narrow"),
        P(None, "narrow"),
        P("narrow", None),
        P("wide", None),
        P("wide"),
        P("wide", None),
        P("wide", None),
    )
    return jax.shard_map(
        functools.partial(on_device, mesh.shape["wide"], mesh.shape["narrow"]),
        mesh=mesh,
        in_specs=placed,
        out_specs=(
            P(("wide", "narrow"), None),
            P(("wide", "narrow"), None),
            P(("wide", "narrow")),
            P("wide", "narrow"),
            P("wide", "narrow"),
            P("wide", "narrow"),
            P("narrow", "wide"),
            P("wide", "narrow"),
            P("wide", "narrow"),
            P(("wide", "narrow")),
            P("wide", "narrow"),
            P("wide", "narrow"),
            P("narrow", "wide"),
        ),
        check_vma=False,
    )
```

profile of v0, /device:TPU:0, one launch (start us, length us, event | category | flops | bytes accessed | tf_op | source)
XLA Modules:
  0.0 507.0 jit_solution(8041697840933142652)
XLA Ops:
  12.7 5.1 %collective-permute-start.10 = (bf16[128,256]{0,1:T(8,128)(2,1)S(1)}, bf16[128,256]{0,1:T(8,128)(2,1)S(1)}, u32[]{:S(2)}, u32[]{:S(2)}) collective-permute-start(bf16[128,256]{0,1:T(8,128)(2,1)S(1)} %dynamic-slice_bitcast_fusion), channel_id=1, source_target_pairs={{0,3},{1,0},{2,1},{3,2},{4,7},{5,4},{6,5},{7,6},{8,11},{9,8},{10,9... | collective-permute-start | bytes 196616 | tf_op jit(solution)/shard_map/ppermute | solution.py:611
  20.3 4.0 collective-permute-done.9
  30.7 33.1 %pair_bias.1 = (s32[2,2048,2048]{2,1,0:T(8,128)}, s16[2048,2048]{1,0:T(8,128)(2,1)}) custom-call(s32[1,4]{1,0:T(1,128)} %len_ref.9, s32[2048,2048]{1,0:T(8,128)} %rel_ref.1, s32[2048,2048]{1,0:T(8,128)} %lay_ref.1, s32[4,128]{1,0:T(4,128)} %bitcast.71, s32[1,2048]{1,0:T(1,128)} %bitcast.70), custom_call_target="tpu_custom_call" | custom-call | flops 4294967296 | bytes 125829120 | tf_op jit(solution)/shard_map/pair_bias/pallas_call | solution.py:119
  63.8 32.4 %all-gather.5.cloned.1.call-done = bf16[2048,1024]{1,0:T(8,128)(2,1)} async-done(((bf16[512,1024]{1,0:T(8,128)(2,1)}), bf16[2048,1024]{1,0:T(8,128)(2,1)}) %all-gather.5.cloned.1.call-update) | async-done | bytes 4194320 | tf_op jit(solution)/shard_map/all_gather | solution.py:656
  97.2 7.7 %convolution_convert_fusion.q_ref.k_ref.v_ref = bf16[2048,768]{1,0:T(8,128)(2,1)} fusion(bf16[2048,1024]{1,0:T(8,128)(2,1)} %all-gather.5.cloned.1.call-done, bf16[1024,768]{1,0:T(8,128)(2,1)} %copy-done.18), kind=kOutput, calls=%fused_computation.6 | convolution fusion | flops 3222798336 | bytes 8912896 | tf_op jit(solution)/shard_map/dot_general | solution.py:19
  104.9 20.8 %attention_forward.2 = (bf16[2048,128]{1,0:T(8,128)(2,1)}, f32[2048,128]{1,0:T(8,128)}, bf16[2,2048,2048]{2,1,0:T(8,128)(2,1)}) custom-call(s32[1,4]{1,0:T(1,128)} %len_ref.9, bf16[2048,768]{1,0:T(8,128)(2,1)} %convolution_convert_fusion.q_ref.k_ref.v_ref, bf16[2048,768]{1,0:T(8,128)(2,1)} %convolution_convert_fusion.q_ref.k_ref.v_ref, ...), custom_call_target="tpu_custom_call" | custom-call | flops 2147483648 | bytes 83886080 | tf_op jit(solution)/shard_map/attention_forward/pallas_call | solution.py:236
  128.2 3.2 collective-permute-start.4
  132.0 20.6 %attention_forward.3 = (bf16[2048,128]{1,0:T(8,128)(2,1)}, f32[2048,128]{1,0:T(8,128)}, bf16[2,2048,2048]{2,1,0:T(8,128)(2,1)}) custom-call(s32[1,4]{1,0:T(1,128)} %len_ref.9, bf16[2048,768]{1,0:T(8,128)(2,1)} %convolution_convert_fusion.q_ref.k_ref.v_ref, bf16[2048,768]{1,0:T(8,128)(2,1)} %convolution_convert_fusion.q_ref.k_ref.v_ref, ...), custom_call_target="tpu_custom_call" | custom-call | flops 2147483648 | bytes 83886080 | tf_op jit(solution)/shard_map/attention_forward/pallas_call | solution.py:236
  152.7 4.6 collective-permute-done.4
  157.2 3.2 collective-permute-done.2
  163.5 3.8 collective-permute-start.7
  177.4 3.3 multiply_reduce_fusion.2
  182.8 9.0 %feed_forward.4 = (bf16[512,704]{1,0:T(8,128)(2,1)}, bf16[512,704]{1,0:T(8,128)(2,1)}, bf16[512,704]{1,0:T(8,128)(2,1)}, f32[512,1024]{1,0:T(8,128)}) custom-call(bf16[512,1024]{1,0:T(8,128)(2,1)} %copy-done.11, bf16[512,1024]{1,0:T(8,128)(2,1)} %refs_2_.5, bf16[704,1024]{1,0:T(8,128)(2,1)} %bitcast.67, bf16[704,1024]{1,0:T(8,128)(2,1)} %bitcast.65, ...), custom_call_target="tpu_custom_call" | custom-call | flops 3690987520 | bytes 10485760 | tf_op jit(solution)/shard_map/feed_forward/pallas_call | solution.py:531
  191.9 13.5 %collective-permute-done.11.x_ref.refs_1_ = bf16[512,1024]{1,0:T(8,128)(2,1)S(1)} collective-permute-done((bf16[512,1024]{1,0:T(8,128)(2,1)S(1)}, bf16[512,1024]{1,0:T(8,128)(2,1)S(1)}, u32[]{:S(2)}, u32[]{:S(2)}) %collective-permute-start.11) | collective-permute-done | bytes 1048608 | tf_op jit(solution)/shard_map/ppermute | solution.py:615
  207.4 9.0 %feed_forward.5 = (bf16[512,704]{1,0:T(8,128)(2,1)}, bf16[512,704]{1,0:T(8,128)(2,1)}, bf16[512,704]{1,0:T(8,128)(2,1)}, f32[512,1024]{1,0:T(8,128)}) custom-call(bf16[512,1024]{1,0:T(8,128)(2,1)} %copy-done.35, bf16[512,1024]{1,0:T(8,128)(2,1)} %collective-permute-done.1.g_ref.refs_3_, bf16[704,1024]{1,0:T(8,128)(2,1)} %bitcast.68, ...), custom_call_target="tpu_custom_call" | custom-call | flops 3690987520 | bytes 10485760 | tf_op jit(solution)/shard_map/feed_forward/pallas_call | solution.py:531
  216.4 9.0 %feed_forward.6 = (bf16[512,704]{1,0:T(8,128)(2,1)}, bf16[512,704]{1,0:T(8,128)(2,1)}, bf16[512,704]{1,0:T(8,128)(2,1)}, f32[512,1024]{1,0:T(8,128)}) custom-call(bf16[512,1024]{1,0:T(8,128)(2,1)} %copy-done.35, bf16[512,1024]{1,0:T(8,128)(2,1)} %collective-permute-done.1.g_ref.refs_3_, bf16[1024,2304]{1,0:T(8,128)(2,1)} %all-gather.9.cloned.1.call-done.refs_0_), custom_call_target="tpu_custom_call" | custom-call | flops 3690987520 | bytes 10485760 | tf_op jit(solution)/shard_map/feed_forward/pallas_call | solution.py:531
  227.9 3.6 add_convert_fusion.2
  233.0 9.0 %feed_forward.7 = (bf16[512,704]{1,0:T(8,128)(2,1)}, bf16[512,704]{1,0:T(8,128)(2,1)}, bf16[512,704]{1,0:T(8,128)(2,1)}, f32[512,1024]{1,0:T(8,128)}) custom-call(bf16[512,1024]{1,0:T(8,128)(2,1)} %copy-done.11, bf16[512,1024]{1,0:T(8,128)(2,1)} %refs_2_.5, bf16[1024,2304]{1,0:T(8,128)(2,1)} %all-gather.9.cloned.1.call-done.refs_0_), custom_call_target="tpu_custom_call" | custom-call | flops 3690987520 | bytes 10485760 | tf_op jit(solution)/shard_map/feed_forward/pallas_call | solution.py:531
  242.0 16.3 %weight_grads.1 = bf16[1024,4608]{1,0:T(8,128)(2,1)} custom-call(bf16[512,1024]{1,0:T(8,128)(2,1)} %copy-done.11, bf16[512,1024]{1,0:T(8,128)(2,1)} %copy-done.35, bf16[512,1024]{1,0:T(8,128)(2,1)} %refs_2_.5, bf16[512,1024]{1,0:T(8,128)(2,1)} %collective-permute-done.1.g_ref.refs_3_, bf16[512,704]{1,0:T(8,128)(2,1)} %get-tuple-element.141.refs_4_, ...), custom_call_target="tpu_custom_call" | custom-call | flops 9663676416 | bytes 27262976 | tf_op jit(solution)/shard_map/weight_grads/pallas_call | solution.py:571
  258.4 3.2 multiply_reduce_fusion.1
  262.4 3.6 fusion.82
  289.9 6.8 %collective-permute-start.19 = (bf16[512,1024]{1,0:T(8,128)(2,1)}, bf16[512,1024]{1,0:T(8,128)(2,1)}, u32[]{:S(2)}, u32[]{:S(2)}) collective-permute-start(bf16[512,1024]{1,0:T(8,128)(2,1)} %add_convert_fusion.1), channel_id=1, source_target_pairs={{0,1},{1,0},{2,3},{3,2},{4,5},{5,4},{6,7},{7,6},{8,9},{9,8},{10,11... | collective-permute-start | bytes 3145736 | tf_op jit(solution)/shard_map/ppermute | solution.py:615
  296.7 35.4 %attention_backward.1 = (bf16[2048,768]{1,0:T(8,128)(2,1)}, bf16[4,2048,2048]{2,1,0:T(8,128)(2,1)}) custom-call(s32[1,4]{1,0:T(1,128)} %len_ref.9, bf16[2048,768]{1,0:T(8,128)(2,1)} %convolution_convert_fusion.q_ref.k_ref.v_ref, bf16[2048,768]{1,0:T(8,128)(2,1)} %convolution_convert_fusion.q_ref.k_ref.v_ref, ...), custom_call_target="tpu_custom_call" | custom-call | flops 8589934592 | bytes 157286400 | tf_op jit(solution)/shard_map/attention_backward/pallas_call | solution.py:366
  332.2 3.7 constant_dynamic-slice_fusion.10
  335.9 3.5 convolution_convert_fusion.2
  341.6 14.6 %reduce-scatter.3.cloned.1.call-done = bf16[128,4608]{1,0:T(8,128)(2,1)} async-done(((bf16[1024,4608]{1,0:T(8,128)(2,1)}), bf16[128,4608]{1,0:T(8,128)(2,1)}) %reduce-scatter.3.cloned.1.call-update) | async-done | bytes 1179664 | tf_op jit(solution)/shard_map/reduce_scatter | solution.py:719
  362.3 44.0 %table_grads.1 = (f32[256,256]{1,0:T(8,128)}, f32[128,256]{1,0:T(8,128)}) custom-call(s32[1,4]{1,0:T(1,128)} %len_ref.9, bf16[4,2048,2048]{2,1,0:T(8,128)(2,1)} %get-tuple-element.175.ds_ref, s16[2048,2048]{1,0:T(8,128)(2,1)} %get-tuple-element.176.code_ref), custom_call_target="tpu_custom_call" | custom-call | flops 8589934592 | bytes 157286400 | tf_op jit(solution)/shard_map/table_grads/pallas_call | solution.py:447
  408.8 3.8 collective-permute-done.21
  413.5 40.1 %collective-permute-done.23 = bf16[128,2304]{1,0:T(8,128)(2,1)} collective-permute-done((bf16[128,2304]{1,0:T(8,128)(2,1)S(1)}, bf16[128,2304]{1,0:T(8,128)(2,1)}, u32[]{:S(2)}, u32[]{:S(2)}) %collective-permute-start.23) | collective-permute-done | bytes 589856 | tf_op jit(solution)/shard_map/ppermute | solution.py:611
  461.6 8.2 %fusion.14 = (f32[512]{0:T(512)S(1)}, f32[512,1024]{1,0:T(8,128)}) fusion(bf16[512,1024]{1,0:T(8,128)(2,1)S(1)} %copy-done.2, f32[1024]{0:T(1024)S(1)} %convert_element_type.123, bf16[1024,3072]{1,0:T(8,128)(2,1)} %all-gather.11.cloned.1.call-done, bf16[512,768]{1,0:T(8,128)(2,1)} %collective-permute-done.22, bf16[512,768]{1,0:T(8,128)(2,1)} %copy-done.38, ...), kind=kOutput, calls=%fused_computation.21 | convolution fusion | flops 3235905024 | bytes 12589056 | tf_op jit(solution)/shard_map/dot_general | solution.py:594
  478.0 4.2 fusion.13
  482.2 3.8 collective-permute-start.26
  (257 shorter events, 105.7 us)
Async XLA Ops:
  7.2 89.0 %all-gather.5.cloned.1.call-start = ((), (), s32[]{:S(2)}) async-start(), calls=%async_computation.2 | async-start | bytes 5242880 | tf_op jit(solution)/shard_map/all_gather | solution.py:656
  12.6 164.7 %all-gather.7.cloned.1.call-start = ((), (), s32[]{:S(2)}) async-start(), calls=%async_computation.3 | async-start | bytes 2359296 | tf_op jit(solution)/shard_map/all_gather | solution.py:670
  25.1 191.4 %all-gather.9.cloned.1.call-start = ((), (), s32[]{:S(2)}) async-start(), calls=%async_computation.4 | async-start | bytes 5308416 | tf_op jit(solution)/shard_map/all_gather | solution.py:688
  96.2 29.5 %collective-permute-start = (bf16[128,2304]{1,0:T(8,128)(2,1)S(1)}, bf16[128,2304]{1,0:T(8,128)(2,1)S(1)}, u32[]{:S(2)}, u32[]{:S(2)}) collective-permute-start(bf16[128,2304]{1,0:T(8,128)(2,1)S(1)} %fusion.24), channel_id=1, source_target_pairs={{0,2},{1,3},{2,0},{3,1},{4,6},{5,7},{6,4},{7,5},{8,10},{9,11},{10,... | collective-permute-start | bytes 1769480 | tf_op jit(solution)/shard_map/ppermute | solution.py:611
  126.6 163.4 %all-gather.11.cloned.1.call-start = ((), (), s32[]{:S(2)}) async-start(), calls=%async_computation.5 | async-start | bytes 7077888 | tf_op jit(solution)/shard_map/all_gather | solution.py:706
  126.6 33.8 %collective-permute-start.1 = (bf16[512,1024]{1,0:T(8,128)(2,1)S(1)}, bf16[512,1024]{1,0:T(8,128)(2,1)}, u32[]{:S(2)}, u32[]{:S(2)}) collective-permute-start(bf16[512,1024]{1,0:T(8,128)(2,1)S(1)} %copy-done.12), channel_id=1, source_target_pairs={{0,1},{1,0},{2,3},{3,2},{4,5},{5,4},{6,7},{7,6},{8,9},{9,8},{10,11... | collective-permute-start | bytes 3145736 | tf_op jit(solution)/shard_map/ppermute | solution.py:615
  128.2 29.1 %collective-permute-start.4 = (bf16[512,128]{1,0:T(8,128)(2,1)S(1)}, bf16[512,128]{1,0:T(8,128)(2,1)S(1)}, u32[]{:S(2)}, u32[]{:S(2)}) collective-permute-start(bf16[512,128]{1,0:T(8,128)(2,1)S(1)} %get-tuple-element.241), channel_id=1, source_target_pairs={{0,3},{1,0},{2,1},{3,2},{4,7},{5,4},{6,5},{7,6},{8,11},{9,8},{10,9... | collective-permute-start | bytes 393224 | tf_op jit(solution)/shard_map/ppermute | solution.py:611
  131.4 25.9 %collective-permute-start.3 = (bf16[512,128]{1,0:T(8,128)(2,1)S(1)}, bf16[512,128]{1,0:T(8,128)(2,1)S(1)}, u32[]{:S(2)}, u32[]{:S(2)}) collective-permute-start(bf16[512,128]{1,0:T(8,128)(2,1)S(1)} %get-tuple-element.242), channel_id=1, source_target_pairs={{0,2},{1,3},{2,0},{3,1},{4,6},{5,7},{6,4},{7,5},{8,10},{9,11},{10,... | collective-permute-start | bytes 393224 | tf_op jit(solution)/shard_map/ppermute | solution.py:611
  131.4 29.1 %collective-permute-start.2 = (bf16[512,128]{1,0:T(8,128)(2,1)S(1)}, bf16[512,128]{1,0:T(8,128)(2,1)S(1)}, u32[]{:S(2)}, u32[]{:S(2)}) collective-permute-start(bf16[512,128]{1,0:T(8,128)(2,1)S(1)} %get-tuple-element.243), channel_id=1, source_target_pairs={{0,1},{1,2},{2,3},{3,0},{4,5},{5,6},{6,7},{7,4},{8,9},{9,10},{10,1... | collective-permute-start | bytes 393224 | tf_op jit(solution)/shard_map/ppermute | solution.py:611
  163.0 8.2 %collective-permute-start.5 = (bf16[512,128]{1,0:T(8,128)(2,1)S(1)}, bf16[512,128]{1,0:T(8,128)(2,1)S(1)}, u32[]{:S(2)}, u32[]{:S(2)}) collective-permute-start(bf16[512,128]{1,0:T(8,128)(2,1)S(1)} %get-tuple-element.239), channel_id=1, source_target_pairs={{0,1},{1,2},{2,3},{3,0},{4,5},{5,6},{6,7},{7,4},{8,9},{9,10},{10,1... | collective-permute-start | bytes 393224 | tf_op jit(solution)/shard_map/ppermute | solution.py:611
  163.5 13.2 %collective-permute-start.7 = (bf16[512,128]{1,0:T(8,128)(2,1)S(1)}, bf16[512,128]{1,0:T(8,128)(2,1)S(1)}, u32[]{:S(2)}, u32[]{:S(2)}) collective-permute-start(bf16[512,128]{1,0:T(8,128)(2,1)S(1)} %get-tuple-element.237), channel_id=1, source_target_pairs={{0,3},{1,0},{2,1},{3,2},{4,7},{5,4},{6,5},{7,6},{8,11},{9,8},{10,9... | collective-permute-start | bytes 393224 | tf_op jit(solution)/shard_map/ppermute | solution.py:611
  167.3 8.0 %collective-permute-start.6 = (bf16[512,128]{1,0:T(8,128)(2,1)S(1)}, bf16[512,128]{1,0:T(8,128)(2,1)S(1)}, u32[]{:S(2)}, u32[]{:S(2)}) collective-permute-start(bf16[512,128]{1,0:T(8,128)(2,1)S(1)} %get-tuple-element.238), channel_id=1, source_target_pairs={{0,2},{1,3},{2,0},{3,1},{4,6},{5,7},{6,4},{7,5},{8,10},{9,11},{10,... | collective-permute-start | bytes 393224 | tf_op jit(solution)/shard_map/ppermute | solution.py:611
  180.9 24.5 %collective-permute-start.11 = (bf16[512,1024]{1,0:T(8,128)(2,1)S(1)}, bf16[512,1024]{1,0:T(8,128)(2,1)S(1)}, u32[]{:S(2)}, u32[]{:S(2)}) collective-permute-start(bf16[512,1024]{1,0:T(8,128)(2,1)S(1)} %multiply_convert_fusion.x_ref.refs_0_), channel_id=1, source_target_pairs={{0,1},{1,0},{2,3},{3,2},{4,5},{5,4},{6,7},{7,6},{8,9},{9,8},{10,11... | collective-permute-start | bytes 3145736 | tf_op jit(solution)/shard_map/ppermute | solution.py:615
  205.4 20.1 %collective-permute-start.14 = (bf16[128,768]{1,0:T(8,128)(2,1)}, bf16[128,768]{1,0:T(8,128)(2,1)}, u32[]{:S(2)}, u32[]{:S(2)}) collective-permute-start(bf16[128,768]{1,0:T(8,128)(2,1)} %constant_dynamic-slice_fusion.14), channel_id=1, source_target_pairs={{0,3},{1,0},{2,1},{3,2},{4,7},{5,4},{6,5},{7,6},{8,11},{9,8},{10,9... | collective-permute-start | bytes 589832 | tf_op jit(solution)/shard_map/ppermute | solution.py:611
  205.4 20.1 %collective-permute-start.13 = (bf16[128,768]{1,0:T(8,128)(2,1)}, bf16[128,768]{1,0:T(8,128)(2,1)}, u32[]{:S(2)}, u32[]{:S(2)}) collective-permute-start(bf16[128,768]{1,0:T(8,128)(2,1)} %constant_dynamic-slice_fusion.14), channel_id=1, source_target_pairs={{0,2},{1,3},{2,0},{3,1},{4,6},{5,7},{6,4},{7,5},{8,10},{9,11},{10,... | collective-permute-start | bytes 589832 | tf_op jit(solution)/shard_map/ppermute | solution.py:611
  207.2 18.3 %collective-permute-start.12 = (bf16[128,768]{1,0:T(8,128)(2,1)}, bf16[128,768]{1,0:T(8,128)(2,1)}, u32[]{:S(2)}, u32[]{:S(2)}) collective-permute-start(bf16[128,768]{1,0:T(8,128)(2,1)} %constant_dynamic-slice_fusion.14), channel_id=1, source_target_pairs={{0,1},{1,2},{2,3},{3,0},{4,5},{5,6},{6,7},{7,4},{8,9},{9,10},{10,1... | collective-permute-start | bytes 589832 | tf_op jit(solution)/shard_map/ppermute | solution.py:611
  227.7 128.4 %reduce-scatter.3.cloned.1.call-start = ((), (), s32[]{:S(2)}) async-start(), calls=%async_computation.6 | async-start | bytes 10616832 | tf_op jit(solution)/shard_map/reduce_scatter | solution.py:719
  231.5 26.8 %collective-permute-start.15 = (bf16[512,1024]{1,0:T(8,128)(2,1)}, bf16[512,1024]{1,0:T(8,128)(2,1)}, u32[]{:S(2)}, u32[]{:S(2)}) collective-permute-start(bf16[512,1024]{1,0:T(8,128)(2,1)} %add_convert_fusion.2), channel_id=1, source_target_pairs={{0,1},{1,0},{2,3},{3,2},{4,5},{5,4},{6,7},{7,6},{8,9},{9,8},{10,11... | collective-permute-start | bytes 3145736 | tf_op jit(solution)/shard_map/ppermute | solution.py:615
  258.3 195.3 %reduce-scatter.5.cloned.1.call-start = ((), (), s32[]{:S(2)}) async-start(), calls=%async_computation.7 | async-start | bytes 4128768 | tf_op jit(solution)/shard_map/reduce_scatter | solution.py:760
  269.2 20.0 %collective-permute-start.18 = (bf16[512,256]{1,0:T(8,128)(2,1)S(1)}, bf16[512,256]{1,0:T(8,128)(2,1)S(1)}, u32[]{:S(2)}, u32[]{:S(2)}) collective-permute-start(bf16[512,256]{1,0:T(8,128)(2,1)S(1)} %get-tuple-element.233), channel_id=1, source_target_pairs={{0,1},{1,2},{2,3},{3,0},{4,5},{5,6},{6,7},{7,4},{8,9},{9,10},{10,1... | collective-permute-start | bytes 786440 | tf_op jit(solution)/shard_map/ppermute | solution.py:611
  269.8 18.7 %collective-permute-start.17 = (bf16[512,256]{1,0:T(8,128)(2,1)S(1)}, bf16[512,256]{1,0:T(8,128)(2,1)S(1)}, u32[]{:S(2)}, u32[]{:S(2)}) collective-permute-start(bf16[512,256]{1,0:T(8,128)(2,1)S(1)} %get-tuple-element.234), channel_id=1, source_target_pairs={{0,2},{1,3},{2,0},{3,1},{4,6},{5,7},{6,4},{7,5},{8,10},{9,11},{10,... | collective-permute-start | bytes 786440 | tf_op jit(solution)/shard_map/ppermute | solution.py:611
  272.8 12.8 %collective-permute-start.16 = (bf16[512,256]{1,0:T(8,128)(2,1)S(1)}, bf16[512,256]{1,0:T(8,128)(2,1)S(1)}, u32[]{:S(2)}, u32[]{:S(2)}) collective-permute-start(bf16[512,256]{1,0:T(8,128)(2,1)S(1)} %get-tuple-element.235), channel_id=1, source_target_pairs={{0,3},{1,0},{2,1},{3,2},{4,7},{5,4},{6,5},{7,6},{8,11},{9,8},{10,9... | collective-permute-start | bytes 786440 | tf_op jit(solution)/shard_map/ppermute | solution.py:611
  289.9 42.2 %collective-permute-start.19 = (bf16[512,1024]{1,0:T(8,128)(2,1)}, bf16[512,1024]{1,0:T(8,128)(2,1)}, u32[]{:S(2)}, u32[]{:S(2)}) collective-permute-start(bf16[512,1024]{1,0:T(8,128)(2,1)} %add_convert_fusion.1), channel_id=1, source_target_pairs={{0,1},{1,0},{2,3},{3,2},{4,5},{5,4},{6,7},{7,6},{8,9},{9,8},{10,11... | collective-permute-start | bytes 3145736 | tf_op jit(solution)/shard_map/ppermute | solution.py:615
  356.3 52.6 %collective-permute-start.20 = (bf16[512,768]{1,0:T(8,128)(2,1)}, bf16[512,768]{1,0:T(8,128)(2,1)S(1)}, u32[]{:S(2)}, u32[]{:S(2)}) collective-permute-start(bf16[512,768]{1,0:T(8,128)(2,1)} %get-tuple-element.180), channel_id=1, source_target_pairs={{0,1},{1,2},{2,3},{3,0},{4,5},{5,6},{6,7},{7,4},{8,9},{9,10},{10,1... | collective-permute-start | bytes 2359304 | tf_op jit(solution)/shard_map/ppermute | solution.py:611
  357.8 54.8 %collective-permute-start.21 = (bf16[512,768]{1,0:T(8,128)(2,1)}, bf16[512,768]{1,0:T(8,128)(2,1)S(1)}, u32[]{:S(2)}, u32[]{:S(2)}) collective-permute-start(bf16[512,768]{1,0:T(8,128)(2,1)} %get-tuple-element.181), channel_id=1, source_target_pairs={{0,2},{1,3},{2,0},{3,1},{4,6},{5,7},{6,4},{7,5},{8,10},{9,11},{10,... | collective-permute-start | bytes 2359304 | tf_op jit(solution)/shard_map/ppermute | solution.py:611
  360.2 52.4 %collective-permute-start.22 = (bf16[512,768]{1,0:T(8,128)(2,1)S(1)}, bf16[512,768]{1,0:T(8,128)(2,1)}, u32[]{:S(2)}, u32[]{:S(2)}) collective-permute-start(bf16[512,768]{1,0:T(8,128)(2,1)S(1)} %copy-done.16), channel_id=1, source_target_pairs={{0,3},{1,0},{2,1},{3,2},{4,7},{5,4},{6,5},{7,6},{8,11},{9,8},{10,9... | collective-permute-start | bytes 2359304 | tf_op jit(solution)/shard_map/ppermute | solution.py:611
  361.7 91.9 %collective-permute-start.23 = (bf16[128,2304]{1,0:T(8,128)(2,1)S(1)}, bf16[128,2304]{1,0:T(8,128)(2,1)}, u32[]{:S(2)}, u32[]{:S(2)}) collective-permute-start(bf16[128,2304]{1,0:T(8,128)(2,1)S(1)} %slice.110), channel_id=1, source_target_pairs={{0,2},{1,3},{2,0},{3,1},{4,6},{5,7},{6,4},{7,5},{8,10},{9,11},{10,... | collective-permute-start | bytes 1769480 | tf_op jit(solution)/shard_map/ppermute | solution.py:611
  469.8 28.3 %collective-permute-start.27 = (bf16[128,256]{1,0:T(8,128)(2,1)S(1)}, bf16[128,256]{1,0:T(8,128)(2,1)S(1)}, u32[]{:S(2)}, u32[]{:S(2)}) collective-permute-start(bf16[128,256]{1,0:T(8,128)(2,1)S(1)} %copy-done.24), channel_id=1, source_target_pairs={{0,3},{1,0},{2,1},{3,2},{4,7},{5,4},{6,5},{7,6},{8,11},{9,8},{10,9... | collective-permute-start | bytes 196616 | tf_op jit(solution)/shard_map/ppermute | solution.py:611
  471.3 26.8 %collective-permute-start.29 = (bf16[128,256]{1,0:T(8,128)(2,1)S(1)}, bf16[128,256]{1,0:T(8,128)(2,1)S(1)}, u32[]{:S(2)}, u32[]{:S(2)}) collective-permute-start(bf16[128,256]{1,0:T(8,128)(2,1)S(1)} %copy-done.23), channel_id=1, source_target_pairs={{0,1},{1,2},{2,3},{3,0},{4,5},{5,6},{6,7},{7,4},{8,9},{9,10},{10,1... | collective-permute-start | bytes 196616 | tf_op jit(solution)/shard_map/ppermute | solution.py:611
  476.6 12.2 %collective-permute-start.30 = (f32[4,12,4]{1,0,2:T(4,128)S(1)}, f32[4,12,4]{1,0,2:T(4,128)S(1)}, u32[]{:S(2)}, u32[]{:S(2)}) collective-permute-start(f32[4,12,4]{1,0,2:T(4,128)S(1)} %fusion.26), channel_id=1, source_target_pairs={{0,16},{4,20},{8,24},{12,28},{16,0},{20,4},{24,8},{28,12},{1,17},{... | collective-permute-start | bytes 2312 | tf_op jit(solution)/shard_map/ppermute | solution.py:776
  482.2 9.6 %collective-permute-start.26 = (f32[2,32]{1,0:T(2,128)S(1)}, f32[2,32]{1,0:T(2,128)S(1)}, u32[]{:S(2)}, u32[]{:S(2)}) collective-permute-start(f32[2,32]{1,0:T(2,128)S(1)} %get-tuple-element.258), channel_id=1, source_target_pairs={{0,3},{1,0},{2,1},{3,2},{4,7},{5,4},{6,5},{7,6},{8,11},{9,8},{10,9... | collective-permute-start | bytes 776 | tf_op jit(solution)/shard_map/ppermute | solution.py:611
  488.9 9.2 %collective-permute-start.28 = (bf16[128,256]{1,0:T(8,128)(2,1)S(1)}, bf16[128,256]{1,0:T(8,128)(2,1)S(1)}, u32[]{:S(2)}, u32[]{:S(2)}) collective-permute-start(bf16[128,256]{1,0:T(8,128)(2,1)S(1)} %copy-done.22), channel_id=1, source_target_pairs={{0,2},{1,3},{2,0},{3,1},{4,6},{5,7},{6,4},{7,5},{8,10},{9,11},{10,... | collective-permute-start | bytes 196616 | tf_op jit(solution)/shard_map/ppermute | solution.py:611
  (53 other events, 451.0 us)
Sparse Core Ops, SparseCore 0:
  12.7 83.4 all-gather.4
  98.7 26.7 all-gather.6
  128.0 38.9 all-gather.8
  227.8 48.3 all-gather.10
  279.6 76.4 reduce-scatter.2
  359.4 48.7 reduce-scatter.4
where the time goes:
time: 517 us; the launch traced here: 507 us
  Pallas kernels  206 us (40%)
  waiting for transfers between devices  131 us (25%)
  starting transfers between devices  48.9 us (9%)
  local copies, waits for them, and re-layouts  37.9 us (7%)
  other arithmetic  34.3 us (7%)
  matrix products  33.7 us (7%)
  between operations  15.3 us (3%)
    ppermute x26, waiting for transfers between devices, along(): lax.ppermute(array, 'narrow', [(i, (i + shift) % ring) for i in range(rin...  67.2 us
    pallas_call x1, Pallas kernels, table_grads(): pl.pallas_call(functools.partial(table_kernel, width=width, parts=parts),...  44 us
    pallas_call x2, Pallas kernels, attention_forward(): pl.pallas_call(functools.partial(forward_kernel, width=width, group=group...  41.4 us
    ppermute x26, starting transfers between devices, along(): lax.ppermute(array, 'narrow', [(i, (i + shift) % ring) for i in range(rin...  37.7 us
    pallas_call x4, Pallas kernels, feed_forward(): pl.pallas_call(functools.partial(feed_forward_kernel, shard is not None),...  36.1 us
    pallas_call x1, Pallas kernels, attention_backward(): pl.pallas_call(functools.partial(backward_kernel, width=width, heads=head...  35.4 us
    pallas_call x1, Pallas kernels, pair_bias(): pl.pallas_call(functools.partial(pair_bias_kernel, width=width, group=gro...  33.1 us
    all_gather x1, waiting for transfers between devices, on_device(): normed_attn_all = lax.all_gather(normed_attn, 'narrow', axis=0, tiled=True)  32.4 us
  transfers between devices with their start and end apart: 39, of which 16 were waited for; matrix products, arithmetic and copies ran while one was open for 15% of the time, Pallas kernels for 41%

commit v1 on v0

--- a/solution.py
+++ b/solution.py
@@ -756,13 +756,12 @@
     mine = leaving[:1] + [along(leaving[d], d, ring) for d in range(1, ring)]
     layer_out = (own_out + other_out.astype(f32)).astype(bf16)
     last_sums = jnp.concatenate([contract_rows(normed_attn_all, d_project).astype(bf16), wout_sums], axis=1)
-    last_sums, ffn_sums = lax.optimization_barrier((last_sums, ffn_sums))
     last_sums = lax.psum_scatter(last_sums, "wide", scatter_dimension=0, tiled=True)
 
     raw_lay, raw_rel = table_grads(page_lengths, d_scores, codes)
+    raw_lay, raw_rel, mine = lax.optimization_barrier((raw_lay, raw_rel, mine))
+    raw_lay, raw_rel, ffn_sums = lax.optimization_barrier((raw_lay, raw_rel, ffn_sums))
     far_sums = [along(ffn_sums[:, 3 * padded * s : 3 * padded * (s + 1)], -2 * s, ring) for s in range(1, shards)]
-    raw_lay, raw_rel, mine, far_sums, last_sums = lax.optimization_barrier(
-        (raw_lay, raw_rel, mine, far_sums, last_sums))
     grad_relative = bucket_sums(raw_rel, heads)
     grad_layout = bucket_sums(raw_lay, heads)
     tables = jnp.concatenate(
@@ -774,6 +773,8 @@
         keep = lax.dynamic_slice_in_dim(tables, bit * reach, reach, 0)
         give = lax.dynamic_slice_in_dim(tables, (1 - bit) * reach, reach, 0)
         tables = keep + lax.ppermute(give, "wide", [(i, i ^ reach) for i in range(wide)])
+        if reach == wide // 2:
+            tables, far_sums, last_sums = lax.optimization_barrier((tables, far_sums, last_sums))
         reach //= 2
     sum_project = last_sums[:, : 3 * head_cols].astype(f32)
     wout_sums = last_sums[:, 3 * head_cols :]

time: 517 us -> 499 us (0.965)
  waiting for transfers between devices: 131 us -> 79.6 us
  Pallas kernels: 206 us -> 228 us
  starting transfers between devices: 48.9 us -> 54.6 us
    ppermute x26, waiting for transfers between devices: 67.2 us -> 35.6 us  [along(): lax.ppermute(array, 'narrow', [(i, (i + shift) % ring) for i in range(rin...]
    reduce_scatter x1, waiting for transfers between devices: 14.6 us -> 0.01 us  [on_device(): ffn_sums = lax.psum_scatter(sums, 'wide', scatter_dimension=0, tiled=True)]
    pallas_call x1, Pallas kernels: 44 us -> 53.1 us  [table_grads(): pl.pallas_call(functools.partial(table_kernel, width=width, parts=parts),...]
    ppermute x26, starting transfers between devices: 37.7 us -> 45.8 us  [along(): lax.ppermute(array, 'narrow', [(i, (i + shift) % ring) for i in range(rin...]
    unnamed x103 -> x95, local copies, waits for them, and re-layouts: 13.8 us -> 12.5 us
  transfers between devices with their start and end apart: 39 -> 39, of which waited for: 16 -> 15; matrix products, arithmetic and copies ran while one was open for 15% -> 19% of each run, Pallas kernels for 41% -> 47%
where the time goes in v1:
time: 499 us; the launch traced here: 490 us
  Pallas kernels  228 us (46%)
  waiting for transfers between devices  79.6 us (16%)
  starting transfers between devices  54.6 us (11%)
  local copies, waits for them, and re-layouts  42.3 us (8%)
  other arithmetic  35.6 us (7%)
  matrix products  34.3 us (7%)
  between operations  15.3 us (3%)
    pallas_call x1, Pallas kernels, table_grads(): pl.pallas_call(functools.partial(table_kernel, width=width, parts=parts),...  53.1 us
    ppermute x26, starting transfers between devices, along(): lax.ppermute(array, 'narrow', [(i, (i + shift) % ring) for i in range(rin...  45.8 us
    pallas_call x2, Pallas kernels, attention_forward(): pl.pallas_call(functools.partial(forward_kernel, width=width, group=group...  45 us
    pallas_call x1, Pallas kernels, attention_backward(): pl.pallas_call(functools.partial(backward_kernel, width=width, heads=head...  40.3 us
    pallas_call x1, Pallas kernels, pair_bias(): pl.pallas_call(functools.partial(pair_bias_kernel, width=width, group=gro...  37.1 us
    pallas_call x4, Pallas kernels, feed_forward(): pl.pallas_call(functools.partial(feed_forward_kernel, shard is not None),...  36.3 us
    ppermute x26, waiting for transfers between devices, along(): lax.ppermute(array, 'narrow', [(i, (i + shift) % ring) for i in range(rin...  35.6 us
    all_gather x1, waiting for transfers between devices, on_device(): normed_attn_all = lax.all_gather(normed_attn, 'narrow', axis=0, tiled=True)  29.3 us
  transfers between devices with their start and end apart: 39, of which 15 were waited for; matrix products, arithmetic and copies ran while one was open for 19% of the time, Pallas kernels for 47%

profile of v1, /device:TPU:0, one launch (start us, length us, event | category | flops | bytes accessed | tf_op | source)
XLA Modules:
  0.0 489.9 jit_solution(8233581698060247898)
XLA Ops:
  12.8 5.1 %collective-permute-start.10 = (bf16[128,256]{0,1:T(8,128)(2,1)S(1)}, bf16[128,256]{0,1:T(8,128)(2,1)S(1)}, u32[]{:S(2)}, u32[]{:S(2)}) collective-permute-start(bf16[128,256]{0,1:T(8,128)(2,1)S(1)} %dynamic-slice_bitcast_fusion), channel_id=1, source_target_pairs={{0,3},{1,0},{2,1},{3,2},{4,7},{5,4},{6,5},{7,6},{8,11},{9,8},{10,9... | collective-permute-start | bytes 196616 | tf_op jit(solution)/shard_map/ppermute | solution.py:611
  20.4 4.0 collective-permute-done.9
  29.8 37.1 %pair_bias.1 = (s32[2,2048,2048]{2,1,0:T(8,128)}, s16[2048,2048]{1,0:T(8,128)(2,1)}) custom-call(s32[1,4]{1,0:T(1,128)} %len_ref.9, s32[2048,2048]{1,0:T(8,128)} %rel_ref.1, s32[2048,2048]{1,0:T(8,128)} %lay_ref.1, s32[4,128]{1,0:T(4,128)} %bitcast.71, s32[1,2048]{1,0:T(1,128)} %bitcast.70), custom_call_target="tpu_custom_call" | custom-call | flops 4294967296 | bytes 125829120 | tf_op jit(solution)/shard_map/pair_bias/pallas_call | solution.py:119
  66.9 29.3 %all-gather.5.cloned.1.call-done = bf16[2048,1024]{1,0:T(8,128)(2,1)} async-done(((bf16[512,1024]{1,0:T(8,128)(2,1)}), bf16[2048,1024]{1,0:T(8,128)(2,1)}) %all-gather.5.cloned.1.call-update) | async-done | bytes 4194320 | tf_op jit(solution)/shard_map/all_gather | solution.py:656
  97.2 7.7 %convolution_convert_fusion.q_ref.k_ref.v_ref = bf16[2048,768]{1,0:T(8,128)(2,1)} fusion(bf16[2048,1024]{1,0:T(8,128)(2,1)} %all-gather.5.cloned.1.call-done, bf16[1024,768]{1,0:T(8,128)(2,1)} %copy-done.19), kind=kOutput, calls=%fused_computation.6 | convolution fusion | flops 3222798336 | bytes 8912896 | tf_op jit(solution)/shard_map/dot_general | solution.py:19
  104.9 22.4 %attention_forward.2 = (bf16[2048,128]{1,0:T(8,128)(2,1)}, f32[2048,128]{1,0:T(8,128)}, bf16[2,2048,2048]{2,1,0:T(8,128)(2,1)}) custom-call(s32[1,4]{1,0:T(1,128)} %len_ref.9, bf16[2048,768]{1,0:T(8,128)(2,1)} %convolution_convert_fusion.q_ref.k_ref.v_ref, bf16[2048,768]{1,0:T(8,128)(2,1)} %convolution_convert_fusion.q_ref.k_ref.v_ref, ...), custom_call_target="tpu_custom_call" | custom-call | flops 2147483648 | bytes 83886080 | tf_op jit(solution)/shard_map/attention_forward/pallas_call | solution.py:236
  129.8 3.2 collective-permute-start.4
  133.6 22.6 %attention_forward.3 = (bf16[2048,128]{1,0:T(8,128)(2,1)}, f32[2048,128]{1,0:T(8,128)}, bf16[2,2048,2048]{2,1,0:T(8,128)(2,1)}) custom-call(s32[1,4]{1,0:T(1,128)} %len_ref.9, bf16[2048,768]{1,0:T(8,128)(2,1)} %convolution_convert_fusion.q_ref.k_ref.v_ref, bf16[2048,768]{1,0:T(8,128)(2,1)} %convolution_convert_fusion.q_ref.k_ref.v_ref, ...), custom_call_target="tpu_custom_call" | custom-call | flops 2147483648 | bytes 83886080 | tf_op jit(solution)/shard_map/attention_forward/pallas_call | solution.py:236
  158.5 3.9 collective-permute-done.2
  165.4 3.8 collective-permute-start.7
  169.9 3.5 collective-permute-done.5
  179.5 3.3 multiply_reduce_fusion.2
  185.0 9.0 %feed_forward.4 = (bf16[512,704]{1,0:T(8,128)(2,1)}, bf16[512,704]{1,0:T(8,128)(2,1)}, bf16[512,704]{1,0:T(8,128)(2,1)}, f32[512,1024]{1,0:T(8,128)}) custom-call(bf16[512,1024]{1,0:T(8,128)(2,1)} %copy-done.11, bf16[512,1024]{1,0:T(8,128)(2,1)} %refs_2_.5, bf16[704,1024]{1,0:T(8,128)(2,1)} %bitcast.67, bf16[704,1024]{1,0:T(8,128)(2,1)} %bitcast.65, ...), custom_call_target="tpu_custom_call" | custom-call | flops 3690987520 | bytes 10485760 | tf_op jit(solution)/shard_map/feed_forward/pallas_call | solution.py:531
  194.0 13.9 %collective-permute-done.11.x_ref.refs_1_ = bf16[512,1024]{1,0:T(8,128)(2,1)S(1)} collective-permute-done((bf16[512,1024]{1,0:T(8,128)(2,1)S(1)}, bf16[512,1024]{1,0:T(8,128)(2,1)S(1)}, u32[]{:S(2)}, u32[]{:S(2)}) %collective-permute-start.11) | collective-permute-done | bytes 1048608 | tf_op jit(solution)/shard_map/ppermute | solution.py:615
  209.9 9.0 %feed_forward.5 = (bf16[512,704]{1,0:T(8,128)(2,1)}, bf16[512,704]{1,0:T(8,128)(2,1)}, bf16[512,704]{1,0:T(8,128)(2,1)}, f32[512,1024]{1,0:T(8,128)}) custom-call(bf16[512,1024]{1,0:T(8,128)(2,1)} %copy-done.34, bf16[512,1024]{1,0:T(8,128)(2,1)} %collective-permute-done.1.g_ref.refs_3_, bf16[704,1024]{1,0:T(8,128)(2,1)} %bitcast.68, ...), custom_call_target="tpu_custom_call" | custom-call | flops 3690987520 | bytes 10485760 | tf_op jit(solution)/shard_map/feed_forward/pallas_call | solution.py:531
  218.9 9.0 %feed_forward.6 = (bf16[512,704]{1,0:T(8,128)(2,1)}, bf16[512,704]{1,0:T(8,128)(2,1)}, bf16[512,704]{1,0:T(8,128)(2,1)}, f32[512,1024]{1,0:T(8,128)}) custom-call(bf16[512,1024]{1,0:T(8,128)(2,1)} %copy-done.34, bf16[512,1024]{1,0:T(8,128)(2,1)} %collective-permute-done.1.g_ref.refs_3_, bf16[1024,2304]{1,0:T(8,128)(2,1)} %all-gather.9.cloned.1.call-done.refs_0_), custom_call_target="tpu_custom_call" | custom-call | flops 3690987520 | bytes 10485760 | tf_op jit(solution)/shard_map/feed_forward/pallas_call | solution.py:531
  230.4 3.6 add_convert_fusion.2
  235.4 9.3 %feed_forward.7 = (bf16[512,704]{1,0:T(8,128)(2,1)}, bf16[512,704]{1,0:T(8,128)(2,1)}, bf16[512,704]{1,0:T(8,128)(2,1)}, f32[512,1024]{1,0:T(8,128)}) custom-call(bf16[512,1024]{1,0:T(8,128)(2,1)} %copy-done.11, bf16[512,1024]{1,0:T(8,128)(2,1)} %refs_2_.5, bf16[1024,2304]{1,0:T(8,128)(2,1)} %all-gather.9.cloned.1.call-done.refs_0_), custom_call_target="tpu_custom_call" | custom-call | flops 3690987520 | bytes 10485760 | tf_op jit(solution)/shard_map/feed_forward/pallas_call | solution.py:531
  244.7 16.3 %weight_grads.1 = bf16[1024,4608]{1,0:T(8,128)(2,1)} custom-call(bf16[512,1024]{1,0:T(8,128)(2,1)} %copy-done.11, bf16[512,1024]{1,0:T(8,128)(2,1)} %copy-done.34, bf16[512,1024]{1,0:T(8,128)(2,1)} %refs_2_.5, bf16[512,1024]{1,0:T(8,128)(2,1)} %collective-permute-done.1.g_ref.refs_3_, bf16[512,704]{1,0:T(8,128)(2,1)} %get-tuple-element.143.refs_4_, ...), custom_call_target="tpu_custom_call" | custom-call | flops 9663676416 | bytes 27262976 | tf_op jit(solution)/shard_map/weight_grads/pallas_call | solution.py:571
  261.1 3.3 multiply_reduce_fusion.1
  265.3 3.6 fusion.82
  292.5 6.2 %collective-permute-start.19 = (bf16[512,1024]{1,0:T(8,128)(2,1)}, bf16[512,1024]{1,0:T(8,128)(2,1)}, u32[]{:S(2)}, u32[]{:S(2)}) collective-permute-start(bf16[512,1024]{1,0:T(8,128)(2,1)} %add_convert_fusion.1), channel_id=1, source_target_pairs={{0,1},{1,0},{2,3},{3,2},{4,5},{5,4},{6,7},{7,6},{8,9},{9,8},{10,11... | collective-permute-start | bytes 3145736 | tf_op jit(solution)/shard_map/ppermute | solution.py:615
  298.7 40.3 %attention_backward.1 = (bf16[2048,768]{1,0:T(8,128)(2,1)}, bf16[4,2048,2048]{2,1,0:T(8,128)(2,1)}) custom-call(s32[1,4]{1,0:T(1,128)} %len_ref.9, bf16[2048,768]{1,0:T(8,128)(2,1)} %convolution_convert_fusion.q_ref.k_ref.v_ref, bf16[2048,768]{1,0:T(8,128)(2,1)} %convolution_convert_fusion.q_ref.k_ref.v_ref, ...), custom_call_target="tpu_custom_call" | custom-call | flops 8589934592 | bytes 157286400 | tf_op jit(solution)/shard_map/attention_backward/pallas_call | solution.py:366
  339.1 4.4 constant_dynamic-slice_fusion.10
  343.5 3.6 convolution_convert_fusion.2
  354.1 53.1 %table_grads.1 = (f32[256,256]{1,0:T(8,128)}, f32[128,256]{1,0:T(8,128)}) custom-call(s32[1,4]{1,0:T(1,128)} %len_ref.9, bf16[4,2048,2048]{2,1,0:T(8,128)(2,1)} %get-tuple-element.177.ds_ref, s16[2048,2048]{1,0:T(8,128)(2,1)} %get-tuple-element.178.code_ref), custom_call_target="tpu_custom_call" | custom-call | flops 8589934592 | bytes 157286400 | tf_op jit(solution)/shard_map/table_grads/pallas_call | solution.py:447
  409.8 7.8 %fusion.14 = (f32[512]{0:T(512)S(1)}, f32[512,1024]{1,0:T(8,128)}) fusion(bf16[512,1024]{1,0:T(8,128)(2,1)S(1)} %copy-done.2, f32[1024]{0:T(1024)S(1)} %convert_element_type.123, bf16[1024,3072]{1,0:T(8,128)(2,1)} %all-gather.11.cloned.1.call-done, bf16[512,768]{1,0:T(8,128)(2,1)} %collective-permute-done.22, ...), kind=kOutput, calls=%fused_computation.21 | convolution fusion | flops 3235905024 | bytes 12589056 | tf_op jit(solution)/shard_map/dot_general | solution.py:594
  422.2 9.0 %collective-permute-start.24 = (bf16[128,2304]{1,0:T(8,128)(2,1)}, bf16[128,2304]{1,0:T(8,128)(2,1)}, u32[]{:S(2)}, u32[]{:S(2)}) collective-permute-start(bf16[128,2304]{1,0:T(8,128)(2,1)} %slice.112), channel_id=1, source_target_pairs={{0,2},{1,3},{2,0},{3,1},{4,6},{5,7},{6,4},{7,5},{8,10},{9,11},{10,... | collective-permute-start | bytes 1769480 | tf_op jit(solution)/shard_map/ppermute | solution.py:611
  440.8 3.5 fusion.13
  444.5 13.2 %collective-permute-done.24 = bf16[128,2304]{1,0:T(8,128)(2,1)} collective-permute-done((bf16[128,2304]{1,0:T(8,128)(2,1)}, bf16[128,2304]{1,0:T(8,128)(2,1)}, u32[]{:S(2)}, u32[]{:S(2)}) %collective-permute-start.24) | collective-permute-done | bytes 589856 | tf_op jit(solution)/shard_map/ppermute | solution.py:611
  461.5 3.5 collective-permute-start.28
  467.3 3.8 collective-permute-start.27
  (247 shorter events, 103.4 us)
Async XLA Ops:
  7.2 89.0 %all-gather.5.cloned.1.call-start = ((), (), s32[]{:S(2)}) async-start(), calls=%async_computation.2 | async-start | bytes 5242880 | tf_op jit(solution)/shard_map/all_gather | solution.py:656
  12.6 166.9 %all-gather.7.cloned.1.call-start = ((), (), s32[]{:S(2)}) async-start(), calls=%async_computation.3 | async-start | bytes 2359296 | tf_op jit(solution)/shard_map/all_gather | solution.py:670
  12.8 7.6 %collective-permute-start.10 = (bf16[128,256]{0,1:T(8,128)(2,1)S(1)}, bf16[128,256]{0,1:T(8,128)(2,1)S(1)}, u32[]{:S(2)}, u32[]{:S(2)}) collective-permute-start(bf16[128,256]{0,1:T(8,128)(2,1)S(1)} %dynamic-slice_bitcast_fusion), channel_id=1, source_target_pairs={{0,3},{1,0},{2,1},{3,2},{4,7},{5,4},{6,5},{7,6},{8,11},{9,8},{10,9... | collective-permute-start | bytes 196616 | tf_op jit(solution)/shard_map/ppermute | solution.py:611
  25.1 193.8 %all-gather.9.cloned.1.call-start = ((), (), s32[]{:S(2)}) async-start(), calls=%async_computation.4 | async-start | bytes 5308416 | tf_op jit(solution)/shard_map/all_gather | solution.py:688
  96.2 31.1 %collective-permute-start = (bf16[128,2304]{1,0:T(8,128)(2,1)S(1)}, bf16[128,2304]{1,0:T(8,128)(2,1)S(1)}, u32[]{:S(2)}, u32[]{:S(2)}) collective-permute-start(bf16[128,2304]{1,0:T(8,128)(2,1)S(1)} %fusion.24), channel_id=1, source_target_pairs={{0,2},{1,3},{2,0},{3,1},{4,6},{5,7},{6,4},{7,5},{8,10},{9,11},{10,... | collective-permute-start | bytes 1769480 | tf_op jit(solution)/shard_map/ppermute | solution.py:611
  128.2 164.4 %all-gather.11.cloned.1.call-start = ((), (), s32[]{:S(2)}) async-start(), calls=%async_computation.5 | async-start | bytes 7077888 | tf_op jit(solution)/shard_map/all_gather | solution.py:706
  128.2 34.2 %collective-permute-start.1 = (bf16[512,1024]{1,0:T(8,128)(2,1)S(1)}, bf16[512,1024]{1,0:T(8,128)(2,1)}, u32[]{:S(2)}, u32[]{:S(2)}) collective-permute-start(bf16[512,1024]{1,0:T(8,128)(2,1)S(1)} %copy-done.12), channel_id=1, source_target_pairs={{0,1},{1,0},{2,3},{3,2},{4,5},{5,4},{6,7},{7,6},{8,9},{9,8},{10,11... | collective-permute-start | bytes 3145736 | tf_op jit(solution)/shard_map/ppermute | solution.py:615
  129.8 28.7 %collective-permute-start.4 = (bf16[512,128]{1,0:T(8,128)(2,1)S(1)}, bf16[512,128]{1,0:T(8,128)(2,1)S(1)}, u32[]{:S(2)}, u32[]{:S(2)}) collective-permute-start(bf16[512,128]{1,0:T(8,128)(2,1)S(1)} %get-tuple-element.245), channel_id=1, source_target_pairs={{0,3},{1,0},{2,1},{3,2},{4,7},{5,4},{6,5},{7,6},{8,11},{9,8},{10,9... | collective-permute-start | bytes 393224 | tf_op jit(solution)/shard_map/ppermute | solution.py:611
  133.0 25.5 %collective-permute-start.3 = (bf16[512,128]{1,0:T(8,128)(2,1)S(1)}, bf16[512,128]{1,0:T(8,128)(2,1)S(1)}, u32[]{:S(2)}, u32[]{:S(2)}) collective-permute-start(bf16[512,128]{1,0:T(8,128)(2,1)S(1)} %get-tuple-element.246), channel_id=1, source_target_pairs={{0,2},{1,3},{2,0},{3,1},{4,6},{5,7},{6,4},{7,5},{8,10},{9,11},{10,... | collective-permute-start | bytes 393224 | tf_op jit(solution)/shard_map/ppermute | solution.py:611
  133.0 29.4 %collective-permute-start.2 = (bf16[512,128]{1,0:T(8,128)(2,1)S(1)}, bf16[512,128]{1,0:T(8,128)(2,1)S(1)}, u32[]{:S(2)}, u32[]{:S(2)}) collective-permute-start(bf16[512,128]{1,0:T(8,128)(2,1)S(1)} %get-tuple-element.247), channel_id=1, source_target_pairs={{0,1},{1,2},{2,3},{3,0},{4,5},{5,6},{6,7},{7,4},{8,9},{9,10},{10,1... | collective-permute-start | bytes 393224 | tf_op jit(solution)/shard_map/ppermute | solution.py:611
  164.9 8.5 %collective-permute-start.5 = (bf16[512,128]{1,0:T(8,128)(2,1)S(1)}, bf16[512,128]{1,0:T(8,128)(2,1)S(1)}, u32[]{:S(2)}, u32[]{:S(2)}) collective-permute-start(bf16[512,128]{1,0:T(8,128)(2,1)S(1)} %get-tuple-element.243), channel_id=1, source_target_pairs={{0,1},{1,2},{2,3},{3,0},{4,5},{5,6},{6,7},{7,4},{8,9},{9,10},{10,1... | collective-permute-start | bytes 393224 | tf_op jit(solution)/shard_map/ppermute | solution.py:611
  165.4 13.4 %collective-permute-start.7 = (bf16[512,128]{1,0:T(8,128)(2,1)S(1)}, bf16[512,128]{1,0:T(8,128)(2,1)S(1)}, u32[]{:S(2)}, u32[]{:S(2)}) collective-permute-start(bf16[512,128]{1,0:T(8,128)(2,1)S(1)} %get-tuple-element.241), channel_id=1, source_target_pairs={{0,3},{1,0},{2,1},{3,2},{4,7},{5,4},{6,5},{7,6},{8,11},{9,8},{10,9... | collective-permute-start | bytes 393224 | tf_op jit(solution)/shard_map/ppermute | solution.py:611
  169.2 8.3 %collective-permute-start.6 = (bf16[512,128]{1,0:T(8,128)(2,1)S(1)}, bf16[512,128]{1,0:T(8,128)(2,1)S(1)}, u32[]{:S(2)}, u32[]{:S(2)}) collective-permute-start(bf16[512,128]{1,0:T(8,128)(2,1)S(1)} %get-tuple-element.242), channel_id=1, source_target_pairs={{0,2},{1,3},{2,0},{3,1},{4,6},{5,7},{6,4},{7,5},{8,10},{9,11},{10,... | collective-permute-start | bytes 393224 | tf_op jit(solution)/shard_map/ppermute | solution.py:611
  183.1 24.8 %collective-permute-start.11 = (bf16[512,1024]{1,0:T(8,128)(2,1)S(1)}, bf16[512,1024]{1,0:T(8,128)(2,1)S(1)}, u32[]{:S(2)}, u32[]{:S(2)}) collective-permute-start(bf16[512,1024]{1,0:T(8,128)(2,1)S(1)} %multiply_convert_fusion.x_ref.refs_0_), channel_id=1, source_target_pairs={{0,1},{1,0},{2,3},{3,2},{4,5},{5,4},{6,7},{7,6},{8,9},{9,8},{10,11... | collective-permute-start | bytes 3145736 | tf_op jit(solution)/shard_map/ppermute | solution.py:615
  207.9 20.1 %collective-permute-start.14 = (bf16[128,768]{1,0:T(8,128)(2,1)}, bf16[128,768]{1,0:T(8,128)(2,1)}, u32[]{:S(2)}, u32[]{:S(2)}) collective-permute-start(bf16[128,768]{1,0:T(8,128)(2,1)} %constant_dynamic-slice_fusion.14), channel_id=1, source_target_pairs={{0,3},{1,0},{2,1},{3,2},{4,7},{5,4},{6,5},{7,6},{8,11},{9,8},{10,9... | collective-permute-start | bytes 589832 | tf_op jit(solution)/shard_map/ppermute | solution.py:611
  207.9 20.1 %collective-permute-start.13 = (bf16[128,768]{1,0:T(8,128)(2,1)}, bf16[128,768]{1,0:T(8,128)(2,1)}, u32[]{:S(2)}, u32[]{:S(2)}) collective-permute-start(bf16[128,768]{1,0:T(8,128)(2,1)} %constant_dynamic-slice_fusion.14), channel_id=1, source_target_pairs={{0,2},{1,3},{2,0},{3,1},{4,6},{5,7},{6,4},{7,5},{8,10},{9,11},{10,... | collective-permute-start | bytes 589832 | tf_op jit(solution)/shard_map/ppermute | solution.py:611
  209.6 18.3 %collective-permute-start.12 = (bf16[128,768]{1,0:T(8,128)(2,1)}, bf16[128,768]{1,0:T(8,128)(2,1)}, u32[]{:S(2)}, u32[]{:S(2)}) collective-permute-start(bf16[128,768]{1,0:T(8,128)(2,1)} %constant_dynamic-slice_fusion.14), channel_id=1, source_target_pairs={{0,1},{1,2},{2,3},{3,0},{4,5},{5,6},{6,7},{7,4},{8,9},{9,10},{10,1... | collective-permute-start | bytes 589832 | tf_op jit(solution)/shard_map/ppermute | solution.py:611
  230.2 188.0 %reduce-scatter.3.cloned.1.call-start = ((), (), s32[]{:S(2)}) async-start(), calls=%async_computation.6 | async-start | bytes 10616832 | tf_op jit(solution)/shard_map/reduce_scatter | solution.py:719
  234.0 27.1 %collective-permute-start.15 = (bf16[512,1024]{1,0:T(8,128)(2,1)}, bf16[512,1024]{1,0:T(8,128)(2,1)}, u32[]{:S(2)}, u32[]{:S(2)}) collective-permute-start(bf16[512,1024]{1,0:T(8,128)(2,1)} %add_convert_fusion.2), channel_id=1, source_target_pairs={{0,1},{1,0},{2,3},{3,2},{4,5},{5,4},{6,7},{7,6},{8,9},{9,8},{10,11... | collective-permute-start | bytes 3145736 | tf_op jit(solution)/shard_map/ppermute | solution.py:615
  261.1 196.7 %reduce-scatter.5.cloned.1.call-start = ((), (), s32[]{:S(2)}) async-start(), calls=%async_computation.7 | async-start | bytes 4128768 | tf_op jit(solution)/shard_map/reduce_scatter | solution.py:759
  272.0 19.8 %collective-permute-start.18 = (bf16[512,256]{1,0:T(8,128)(2,1)S(1)}, bf16[512,256]{1,0:T(8,128)(2,1)S(1)}, u32[]{:S(2)}, u32[]{:S(2)}) collective-permute-start(bf16[512,256]{1,0:T(8,128)(2,1)S(1)} %get-tuple-element.237), channel_id=1, source_target_pairs={{0,1},{1,2},{2,3},{3,0},{4,5},{5,6},{6,7},{7,4},{8,9},{9,10},{10,1... | collective-permute-start | bytes 786440 | tf_op jit(solution)/shard_map/ppermute | solution.py:611
  272.3 18.8 %collective-permute-start.17 = (bf16[512,256]{1,0:T(8,128)(2,1)S(1)}, bf16[512,256]{1,0:T(8,128)(2,1)S(1)}, u32[]{:S(2)}, u32[]{:S(2)}) collective-permute-start(bf16[512,256]{1,0:T(8,128)(2,1)S(1)} %get-tuple-element.238), channel_id=1, source_target_pairs={{0,2},{1,3},{2,0},{3,1},{4,6},{5,7},{6,4},{7,5},{8,10},{9,11},{10,... | collective-permute-start | bytes 786440 | tf_op jit(solution)/shard_map/ppermute | solution.py:611
  275.2 12.8 %collective-permute-start.16 = (bf16[512,256]{1,0:T(8,128)(2,1)S(1)}, bf16[512,256]{1,0:T(8,128)(2,1)S(1)}, u32[]{:S(2)}, u32[]{:S(2)}) collective-permute-start(bf16[512,256]{1,0:T(8,128)(2,1)S(1)} %get-tuple-element.239), channel_id=1, source_target_pairs={{0,3},{1,0},{2,1},{3,2},{4,7},{5,4},{6,5},{7,6},{8,11},{9,8},{10,9... | collective-permute-start | bytes 786440 | tf_op jit(solution)/shard_map/ppermute | solution.py:611
  292.5 46.6 %collective-permute-start.19 = (bf16[512,1024]{1,0:T(8,128)(2,1)}, bf16[512,1024]{1,0:T(8,128)(2,1)}, u32[]{:S(2)}, u32[]{:S(2)}) collective-permute-start(bf16[512,1024]{1,0:T(8,128)(2,1)} %add_convert_fusion.1), channel_id=1, source_target_pairs={{0,1},{1,0},{2,3},{3,2},{4,5},{5,4},{6,7},{7,6},{8,9},{9,8},{10,11... | collective-permute-start | bytes 3145736 | tf_op jit(solution)/shard_map/ppermute | solution.py:615
  349.3 60.4 %collective-permute-start.20 = (bf16[512,768]{1,0:T(8,128)(2,1)}, bf16[512,768]{1,0:T(8,128)(2,1)S(1)}, u32[]{:S(2)}, u32[]{:S(2)}) collective-permute-start(bf16[512,768]{1,0:T(8,128)(2,1)} %get-tuple-element.182), channel_id=1, source_target_pairs={{0,1},{1,2},{2,3},{3,0},{4,5},{5,6},{6,7},{7,4},{8,9},{9,10},{10,1... | collective-permute-start | bytes 2359304 | tf_op jit(solution)/shard_map/ppermute | solution.py:611
  350.4 59.4 %collective-permute-start.21 = (bf16[512,768]{1,0:T(8,128)(2,1)S(1)}, bf16[512,768]{1,0:T(8,128)(2,1)S(1)}, u32[]{:S(2)}, u32[]{:S(2)}) collective-permute-start(bf16[512,768]{1,0:T(8,128)(2,1)S(1)} %copy-done.17), channel_id=1, source_target_pairs={{0,2},{1,3},{2,0},{3,1},{4,6},{5,7},{6,4},{7,5},{8,10},{9,11},{10,... | collective-permute-start | bytes 2359304 | tf_op jit(solution)/shard_map/ppermute | solution.py:611
  352.1 57.7 %collective-permute-start.22 = (bf16[512,768]{1,0:T(8,128)(2,1)S(1)}, bf16[512,768]{1,0:T(8,128)(2,1)}, u32[]{:S(2)}, u32[]{:S(2)}) collective-permute-start(bf16[512,768]{1,0:T(8,128)(2,1)S(1)} %copy-done.16), channel_id=1, source_target_pairs={{0,3},{1,0},{2,1},{3,2},{4,7},{5,4},{6,5},{7,6},{8,11},{9,8},{10,9... | collective-permute-start | bytes 2359304 | tf_op jit(solution)/shard_map/ppermute | solution.py:611
  422.2 35.5 %collective-permute-start.24 = (bf16[128,2304]{1,0:T(8,128)(2,1)}, bf16[128,2304]{1,0:T(8,128)(2,1)}, u32[]{:S(2)}, u32[]{:S(2)}) collective-permute-start(bf16[128,2304]{1,0:T(8,128)(2,1)} %slice.112), channel_id=1, source_target_pairs={{0,2},{1,3},{2,0},{3,1},{4,6},{5,7},{6,4},{7,5},{8,10},{9,11},{10,... | collective-permute-start | bytes 1769480 | tf_op jit(solution)/shard_map/ppermute | solution.py:611
  461.4 15.6 %collective-permute-start.31 = (f32[2,12,4]{1,0,2:T(2,128)S(1)}, f32[2,12,4]{1,0,2:T(2,128)S(1)}, u32[]{:S(2)}, u32[]{:S(2)}) collective-permute-start(f32[2,12,4]{1,0,2:T(2,128)S(1)} %constant_dynamic-slice_fusion.3), channel_id=1, source_target_pairs={{0,8},{4,12},{8,0},{12,4},{16,24},{20,28},{24,16},{28,20},{1,9},{5... | collective-permute-start | bytes 1160 | tf_op jit(solution)/shard_map/ppermute | solution.py:775
  461.5 18.1 %collective-permute-start.28 = (bf16[128,256]{1,0:T(8,128)(2,1)}, bf16[128,256]{1,0:T(8,128)(2,1)S(1)}, u32[]{:S(2)}, u32[]{:S(2)}) collective-permute-start(bf16[128,256]{1,0:T(8,128)(2,1)} %get-tuple-element.249), channel_id=1, source_target_pairs={{0,3},{1,0},{2,1},{3,2},{4,7},{5,4},{6,5},{7,6},{8,11},{9,8},{10,9... | collective-permute-start | bytes 196616 | tf_op jit(solution)/shard_map/ppermute | solution.py:611
  467.3 6.5 %collective-permute-start.25 = (f32[2,32]{1,0:T(2,128)S(1)}, f32[2,32]{1,0:T(2,128)S(1)}, u32[]{:S(2)}, u32[]{:S(2)}) collective-permute-start(f32[2,32]{1,0:T(2,128)S(1)} %get-tuple-element.261), channel_id=1, source_target_pairs={{0,1},{1,2},{2,3},{3,0},{4,5},{5,6},{6,7},{7,4},{8,9},{9,10},{10,1... | collective-permute-start | bytes 776 | tf_op jit(solution)/shard_map/ppermute | solution.py:611
  467.3 7.1 %collective-permute-start.27 = (f32[2,32]{1,0:T(2,128)S(1)}, f32[2,32]{1,0:T(2,128)S(1)}, u32[]{:S(2)}, u32[]{:S(2)}) collective-permute-start(f32[2,32]{1,0:T(2,128)S(1)} %get-tuple-element.262), channel_id=1, source_target_pairs={{0,3},{1,0},{2,1},{3,2},{4,7},{5,4},{6,5},{7,6},{8,11},{9,8},{10,9... | collective-permute-start | bytes 776 | tf_op jit(solution)/shard_map/ppermute | solution.py:611
  (47 other events, 940.0 us)
Sparse Core Ops, SparseCore 0:
  12.7 83.4 all-gather.4
  98.7 26.7 all-gather.6
  128.3 38.6 all-gather.8
  230.3 46.0 all-gather.10
  279.7 76.4 reduce-scatter.2
  359.6 48.7 reduce-scatter.4

commit v2 on v1

--- a/solution.py
+++ b/solution.py
@@ -397,7 +397,32 @@
     )(page_lengths, proj, proj, proj, d_att, *exps, *atts, *rinvs)
 
 
-def table_kernel(len_ref, ds_ref, code_ref, hl_ref, hr_ref, *bufs, width, parts):
+def parity_sign(v):
+    v = v ^ (v >> 2)
+    v = v ^ (v >> 1)
+    return (1 - 2 * (v & 1)).astype(f32)
+
+
+def bucket_totals(raw, first, heads):
+    rows, cols = raw.shape
+    low = rows // (16 * heads)
+    r = lax.broadcasted_iota(jnp.int32, raw.shape, 0)
+    c = lax.broadcasted_iota(jnp.int32, raw.shape, 1)
+    kept = jnp.where((r & 15) == (c & 15), raw, 0.0)
+    c = lax.broadcasted_iota(jnp.int32, (cols, 128), 0)
+    y = lax.broadcasted_iota(jnp.int32, (cols, 128), 1)
+    right = jnp.where(y < cols // 16, parity_sign((c >> 4) & y), 0.0)
+    r = lax.broadcasted_iota(jnp.int32, (low * heads, rows), 1) >> 4
+    x = lax.broadcasted_iota(jnp.int32, (low * heads, rows), 0)
+    function = (r // heads + first) & (low - 1)
+    left = jnp.where(r % heads == x % heads, parity_sign(function & (x // heads)), 0.0)
+    exact = lax.Precision.HIGHEST
+    half = lax.dot_general(kept, right, NN, precision=exact, preferred_element_type=f32)
+    out = lax.dot_general(left, half, NN, precision=exact, preferred_element_type=f32)
+    return out * f32(1.0 / (low * (cols // 16)))
+
+
+def table_kernel(len_ref, ds_ref, code_ref, out_ref, hl_ref, hr_ref, *bufs, width, parts):
     heads, tq, count = ds_ref.shape
     i = pl.program_id(0)
     t0 = i * tq
@@ -439,6 +464,12 @@
 
     lax.fori_loop(0, steps, chunk, 0)
 
+    @pl.when(i == pl.num_programs(0) - 1)
+    def _():
+        out_ref[...] = jnp.zeros_like(out_ref)
+        out_ref[:4 * heads, :] = bucket_totals(hl_ref[...], 1, heads)
+        out_ref[4 * heads:6 * heads, :] = bucket_totals(hr_ref[...], 0, heads)
+
 
 def table_grads(page_lengths, ds, code, tq=256, width=256, parts=2):
     heads, count, _ = ds.shape
@@ -452,15 +483,9 @@
             pl.BlockSpec((heads, tq, count), lambda i: (0, i, 0)),
             pl.BlockSpec((tq, count), lambda i: (i, 0)),
         ],
-        out_specs=[
-            pl.BlockSpec((64 * heads, 256), fixed),
-            pl.BlockSpec((32 * heads, 256), fixed),
-        ],
-        out_shape=[
-            jax.ShapeDtypeStruct((64 * heads, 256), f32),
-            jax.ShapeDtypeStruct((32 * heads, 256), f32),
-        ],
-        scratch_shapes=[
+        out_specs=pl.BlockSpec((8 * heads, 128), fixed),
+        out_shape=jax.ShapeDtypeStruct((8 * heads, 128), f32),
+        scratch_shapes=[pltpu.VMEM((64 * heads, 256), f32), pltpu.VMEM((32 * heads, 256), f32)] + [
             pltpu.VMEM((80 * heads, deep), bf16),
             pltpu.VMEM((256, deep), bf16),
             pltpu.VMEM((256, deep), bf16),
@@ -472,21 +497,9 @@
     )(page_lengths, ds, code)
 
 
-def bucket_sums(raw, heads):
-    right = raw.shape[1] // 16
-    left = raw.shape[0] // (16 * heads)
-    cube = raw.reshape(left, heads, 16, right, 16)
-    traced = jnp.sum(cube * jnp.eye(16, dtype=f32)[None, None, :, None, :], axis=(2, 4))
-    if left == 4:
-        traced = jnp.concatenate([traced[3:], traced[:3]], axis=0)
-
-    def table(n):
-        v = lax.iota(jnp.int32, n)
-        both = v[:, None] & v[None, :]
-        return (1 - 2 * (lax.population_count(both) & 1)).astype(f32)
-
-    out = jnp.einsum("ahn,ax,ny->yxh", traced, table(left), table(right), precision=lax.Precision.HIGHEST)
-    return out.reshape(left * right, heads) / (left * right)
+def bucket_sums(totals, heads, first, low):
+    rows = totals[first * heads:(first + low) * heads, :16].reshape(low, heads, 16)
+    return jnp.transpose(rows, (2, 0, 1)).reshape(16 * low, heads)
 
 
 TANH_SLOPE = 0.7978845608028654
@@ -698,13 +711,9 @@
     near = (w_gate.T, w_up.T, down_projection_weight)
     shards = ring // 2
     own = [feed_forward(normed_ffn, out_grad, units, near)]
-    own, other_normed, late_project = lax.optimization_barrier((own, other_normed, own_rows_project))
-    project_pieces = [along(late_project, d, ring) for d in range(1, ring)]
+    own, other_normed = lax.optimization_barrier((own, other_normed))
     other = [feed_forward(other_normed, other_grad, units, near)]
     other += [feed_forward(other_normed, other_grad, units, (far,), s) for s in range(shards - 1)]
-    other, project_pieces = lax.optimization_barrier((other, project_pieces))
-    w_project_all = lax.all_gather(
-        jnp.concatenate([own_rows_project] + project_pieces, axis=1), "wide", axis=0, tiled=True)
     other_d_normed = sum(o[3] for o in other).astype(bf16)
     late_normed, other_d_normed = lax.optimization_barrier((normed_ffn, other_d_normed))
     other_d_normed = swap(other_d_normed, ring)
@@ -744,13 +753,16 @@
         own_out = own_out + dot(own_hidden[s], down, dims)
         other_out = other_out + dot(other_hidden[s], down, dims)
     own_out = own_out + middle
-    wout_sums, d_attended, w_project_all, own_out, other_out = lax.optimization_barrier(
-        (wout_sums, d_attended, w_project_all, own_out, other_out.astype(bf16)))
+    wout_sums, d_attended, own_out, other_out, late_project = lax.optimization_barrier(
+        (wout_sums, d_attended, own_out, other_out.astype(bf16), own_rows_project))
     other_out = swap(other_out, ring)
+    project_pieces = [along(late_project, d, ring) for d in range(1, ring)]
 
     d_project, d_scores = attention_backward(
         page_lengths, projected, [r[2] for r in results], d_attended, attended, [r[1] for r in results])
-    d_project, other_out = lax.optimization_barrier((d_project, other_out))
+    d_project, other_out, project_pieces = lax.optimization_barrier((d_project, other_out, project_pieces))
+    w_project_all = lax.all_gather(
+        jnp.concatenate([own_rows_project] + project_pieces, axis=1), "wide", axis=0, tiled=True)
     leaving = [rows_of(d_project, (me + d) % ring, tokens) for d in range(ring)]
     leaving, d_project, own_out = lax.optimization_barrier((leaving, d_project, own_out))
     mine = leaving[:1] + [along(leaving[d], d, ring) for d in range(1, ring)]
@@ -758,12 +770,11 @@
     last_sums = jnp.concatenate([contract_rows(normed_attn_all, d_project).astype(bf16), wout_sums], axis=1)
     last_sums = lax.psum_scatter(last_sums, "wide", scatter_dimension=0, tiled=True)
 
-    raw_lay, raw_rel = table_grads(page_lengths, d_scores, codes)
-    raw_lay, raw_rel, mine = lax.optimization_barrier((raw_lay, raw_rel, mine))
-    raw_lay, raw_rel, ffn_sums = lax.optimization_barrier((raw_lay, raw_rel, ffn_sums))
+    totals = table_grads(page_lengths, d_scores, codes)
     far_sums = [along(ffn_sums[:, 3 * padded * s : 3 * padded * (s + 1)], -2 * s, ring) for s in range(1, shards)]
-    grad_relative = bucket_sums(raw_rel, heads)
-    grad_layout = bucket_sums(raw_lay, heads)
+    totals, mine, far_sums = lax.optimization_barrier((totals, mine, far_sums))
+    grad_relative = bucket_sums(totals, heads, 4, 2)
+    grad_layout = bucket_sums(totals, heads, 0, 4)
     tables = jnp.concatenate(
         [grad_relative.reshape(wide, -1, heads), grad_layout.reshape(wide, -1, heads)], axis=1)
     n_rel = grad_relative.shape[0] // wide
@@ -774,7 +785,7 @@
         give = lax.dynamic_slice_in_dim(tables, (1 - bit) * reach, reach, 0)
         tables = keep + lax.ppermute(give, "wide", [(i, i ^ reach) for i in range(wide)])
         if reach == wide // 2:
-            tables, far_sums, last_sums = lax.optimization_barrier((tables, far_sums, last_sums))
+            tables, last_sums = lax.optimization_barrier((tables, last_sums))
         reach //= 2
     sum_project = last_sums[:, : 3 * head_cols].astype(f32)
     wout_sums = last_sums[:, 3 * head_cols :]

time: 499 us -> 503 us (level)
  waiting for transfers between devices: 79.6 us -> 112 us
  Pallas kernels: 228 us -> 217 us
  local copies, waits for them, and re-layouts: 42.3 us -> 32.6 us
    ppermute x26, waiting for transfers between devices: 35.6 us -> 65.7 us  [along(): lax.ppermute(array, 'narrow', [(i, (i + shift) % ring) for i in range(rin...]
    ppermute x3, starting transfers between devices: 0.15 us -> 5.3 us  [on_device(): lax.ppermute(give, 'wide', [(i, i ^ reach) for i in range(wide)])]
    unnamed x95 -> x103, local copies, waits for them, and re-layouts: 12.5 us -> 14.4 us
  transfers between devices with their start and end apart: 39 -> 39, of which waited for: 15 -> 15; matrix products, arithmetic and copies ran while one was open for 19% -> 16% of each run, Pallas kernels for 47% -> 42%
where the time goes in v2:
time: 503 us; the launch traced here: 499 us
  Pallas kernels  217 us (43%)
  waiting for transfers between devices  112 us (22%)
  starting transfers between devices  56.5 us (11%)
  matrix products  34.4 us (7%)
  local copies, waits for them, and re-layouts  32.6 us (6%)
  other arithmetic  31.6 us (6%)
  between operations  15.1 us (3%)
    ppermute x26, waiting for transfers between devices, along(): lax.ppermute(array, 'narrow', [(i, (i + shift) % ring) for i in range(rin...  65.7 us
    pallas_call x1, Pallas kernels, table_grads(): pl.pallas_call(functools.partial(table_kernel, width=width, parts=parts),...  49.9 us
    ppermute x26, starting transfers between devices, along(): lax.ppermute(array, 'narrow', [(i, (i + shift) % ring) for i in range(rin...  43.6 us
    pallas_call x2, Pallas kernels, attention_forward(): pl.pallas_call(functools.partial(forward_kernel, width=width, group=group...  42.3 us
    pallas_call x1, Pallas kernels, attention_backward(): pl.pallas_call(functools.partial(backward_kernel, width=width, heads=head...  37.3 us
    pallas_call x4, Pallas kernels, feed_forward(): pl.pallas_call(functools.partial(feed_forward_kernel, shard is not None),...  36.1 us
    pallas_call x1, Pallas kernels, pair_bias(): pl.pallas_call(functools.partial(pair_bias_kernel, width=width, group=gro...  34.7 us
    all_gather x1, waiting for transfers between devices, on_device(): normed_attn_all = lax.all_gather(normed_attn, 'narrow', axis=0, tiled=True)  30.8 us
  transfers between devices with their start and end apart: 39, of which 15 were waited for; matrix products, arithmetic and copies ran while one was open for 16% of the time, Pallas kernels for 42%

profile of v2, /device:TPU:0, one launch (start us, length us, event | category | flops | bytes accessed | tf_op | source)
XLA Modules:
  0.0 498.6 jit_solution(12795201796178890141)
XLA Ops:
  13.3 5.1 %collective-permute-start.10 = (bf16[128,256]{0,1:T(8,128)(2,1)S(1)}, bf16[128,256]{0,1:T(8,128)(2,1)S(1)}, u32[]{:S(2)}, u32[]{:S(2)}) collective-permute-start(bf16[128,256]{0,1:T(8,128)(2,1)S(1)} %dynamic-slice_bitcast_fusion), channel_id=1, source_target_pairs={{0,3},{1,0},{2,1},{3,2},{4,7},{5,4},{6,5},{7,6},{8,11},{9,8},{10,9... | collective-permute-start | bytes 196616 | tf_op jit(solution)/shard_map/ppermute | solution.py:624
  20.9 4.0 collective-permute-done.9
  31.3 34.7 %pair_bias.1 = (s32[2,2048,2048]{2,1,0:T(8,128)}, s16[2048,2048]{1,0:T(8,128)(2,1)}) custom-call(s32[1,4]{1,0:T(1,128)} %len_ref.9, s32[2048,2048]{1,0:T(8,128)} %rel_ref.1, s32[2048,2048]{1,0:T(8,128)} %lay_ref.1, s32[4,128]{1,0:T(4,128)} %bitcast.68, s32[1,2048]{1,0:T(1,128)} %bitcast.67), custom_call_target="tpu_custom_call" | custom-call | flops 4294967296 | bytes 125829120 | tf_op jit(solution)/shard_map/pair_bias/pallas_call | solution.py:119
  66.0 30.8 %all-gather.5.cloned.1.call-done = bf16[2048,1024]{1,0:T(8,128)(2,1)} async-done(((bf16[512,1024]{1,0:T(8,128)(2,1)}), bf16[2048,1024]{1,0:T(8,128)(2,1)}) %all-gather.5.cloned.1.call-update) | async-done | bytes 4194320 | tf_op jit(solution)/shard_map/all_gather | solution.py:669
  97.8 7.9 %convolution_convert_fusion.q_ref.k_ref.v_ref = bf16[2048,768]{1,0:T(8,128)(2,1)} fusion(bf16[2048,1024]{1,0:T(8,128)(2,1)} %all-gather.5.cloned.1.call-done, bf16[1024,768]{1,0:T(8,128)(2,1)} %copy-done.20), kind=kOutput, calls=%fused_computation.6 | convolution fusion | flops 3222798336 | bytes 8912896 | tf_op jit(solution)/shard_map/dot_general | solution.py:19
  105.7 21.3 %attention_forward.2 = (bf16[2048,128]{1,0:T(8,128)(2,1)}, f32[2048,128]{1,0:T(8,128)}, bf16[2,2048,2048]{2,1,0:T(8,128)(2,1)}) custom-call(s32[1,4]{1,0:T(1,128)} %len_ref.9, bf16[2048,768]{1,0:T(8,128)(2,1)} %convolution_convert_fusion.q_ref.k_ref.v_ref, bf16[2048,768]{1,0:T(8,128)(2,1)} %convolution_convert_fusion.q_ref.k_ref.v_ref, ...), custom_call_target="tpu_custom_call" | custom-call | flops 2147483648 | bytes 83886080 | tf_op jit(solution)/shard_map/attention_forward/pallas_call | solution.py:236
  129.1 3.2 collective-permute-start.4
  133.0 21.0 %attention_forward.3 = (bf16[2048,128]{1,0:T(8,128)(2,1)}, f32[2048,128]{1,0:T(8,128)}, bf16[2,2048,2048]{2,1,0:T(8,128)(2,1)}) custom-call(s32[1,4]{1,0:T(1,128)} %len_ref.9, bf16[2048,768]{1,0:T(8,128)(2,1)} %convolution_convert_fusion.q_ref.k_ref.v_ref, bf16[2048,768]{1,0:T(8,128)(2,1)} %convolution_convert_fusion.q_ref.k_ref.v_ref, ...), custom_call_target="tpu_custom_call" | custom-call | flops 2147483648 | bytes 83886080 | tf_op jit(solution)/shard_map/attention_forward/pallas_call | solution.py:236
  154.0 4.0 collective-permute-done.4
  158.0 4.3 collective-permute-done.2
  164.8 9.4 %collective-permute-start.5 = (bf16[512,128]{1,0:T(8,128)(2,1)S(1)}, bf16[512,128]{1,0:T(8,128)(2,1)S(1)}, u32[]{:S(2)}, u32[]{:S(2)}) collective-permute-start(bf16[512,128]{1,0:T(8,128)(2,1)S(1)} %get-tuple-element.213), channel_id=1, source_target_pairs={{0,1},{1,2},{2,3},{3,0},{4,5},{5,6},{6,7},{7,4},{8,9},{9,10},{10,1... | collective-permute-start | bytes 393224 | tf_op jit(solution)/shard_map/ppermute | solution.py:624
  174.3 3.8 collective-permute-start.7
  178.8 3.8 collective-permute-done.5
  188.9 3.3 multiply_reduce_fusion.1
  193.4 9.0 %feed_forward.4 = (bf16[512,704]{1,0:T(8,128)(2,1)}, bf16[512,704]{1,0:T(8,128)(2,1)}, bf16[512,704]{1,0:T(8,128)(2,1)}, f32[512,1024]{1,0:T(8,128)}) custom-call(bf16[512,1024]{1,0:T(8,128)(2,1)} %copy-done.13, bf16[512,1024]{1,0:T(8,128)(2,1)} %refs_2_.5, bf16[704,1024]{1,0:T(8,128)(2,1)} %bitcast.63, bf16[704,1024]{1,0:T(8,128)(2,1)} %bitcast.61, ...), custom_call_target="tpu_custom_call" | custom-call | flops 3690987520 | bytes 10485760 | tf_op jit(solution)/shard_map/feed_forward/pallas_call | solution.py:544
  202.4 14.7 %collective-permute-done.11.x_ref.refs_1_ = bf16[512,1024]{1,0:T(8,128)(2,1)S(1)} collective-permute-done((bf16[512,1024]{1,0:T(8,128)(2,1)S(1)}, bf16[512,1024]{1,0:T(8,128)(2,1)S(1)}, u32[]{:S(2)}, u32[]{:S(2)}) %collective-permute-start.11) | collective-permute-done | bytes 1048608 | tf_op jit(solution)/shard_map/ppermute | solution.py:628
  218.0 9.0 %feed_forward.5 = (bf16[512,704]{1,0:T(8,128)(2,1)}, bf16[512,704]{1,0:T(8,128)(2,1)}, bf16[512,704]{1,0:T(8,128)(2,1)}, f32[512,1024]{1,0:T(8,128)}) custom-call(bf16[512,1024]{1,0:T(8,128)(2,1)} %copy-done.38, bf16[512,1024]{1,0:T(8,128)(2,1)} %collective-permute-done.1.g_ref.refs_3_, bf16[704,1024]{1,0:T(8,128)(2,1)} %bitcast.64, ...), custom_call_target="tpu_custom_call" | custom-call | flops 3690987520 | bytes 10485760 | tf_op jit(solution)/shard_map/feed_forward/pallas_call | solution.py:544
  226.9 9.2 %feed_forward.6 = (bf16[512,704]{1,0:T(8,128)(2,1)}, bf16[512,704]{1,0:T(8,128)(2,1)}, bf16[512,704]{1,0:T(8,128)(2,1)}, f32[512,1024]{1,0:T(8,128)}) custom-call(bf16[512,1024]{1,0:T(8,128)(2,1)} %copy-done.38, bf16[512,1024]{1,0:T(8,128)(2,1)} %collective-permute-done.1.g_ref.refs_3_, bf16[1024,2304]{1,0:T(8,128)(2,1)} %all-gather.9.cloned.1.call-done.refs_0_), custom_call_target="tpu_custom_call" | custom-call | flops 3690987520 | bytes 10485760 | tf_op jit(solution)/shard_map/feed_forward/pallas_call | solution.py:544
  236.1 2.9 add_convert_fusion.2
  239.3 9.0 %feed_forward.7 = (bf16[512,704]{1,0:T(8,128)(2,1)}, bf16[512,704]{1,0:T(8,128)(2,1)}, bf16[512,704]{1,0:T(8,128)(2,1)}, f32[512,1024]{1,0:T(8,128)}) custom-call(bf16[512,1024]{1,0:T(8,128)(2,1)} %copy-done.13, bf16[512,1024]{1,0:T(8,128)(2,1)} %refs_2_.5, bf16[1024,2304]{1,0:T(8,128)(2,1)} %all-gather.9.cloned.1.call-done.refs_0_), custom_call_target="tpu_custom_call" | custom-call | flops 3690987520 | bytes 10485760 | tf_op jit(solution)/shard_map/feed_forward/pallas_call | solution.py:544
  248.4 16.3 %weight_grads.1 = bf16[1024,4608]{1,0:T(8,128)(2,1)} custom-call(bf16[512,1024]{1,0:T(8,128)(2,1)} %copy-done.13, bf16[512,1024]{1,0:T(8,128)(2,1)} %copy-done.38, bf16[512,1024]{1,0:T(8,128)(2,1)} %refs_2_.5, bf16[512,1024]{1,0:T(8,128)(2,1)} %collective-permute-done.1.g_ref.refs_3_, bf16[512,704]{1,0:T(8,128)(2,1)} %get-tuple-element.119.refs_4_, ...), custom_call_target="tpu_custom_call" | custom-call | flops 9663676416 | bytes 27262976 | tf_op jit(solution)/shard_map/weight_grads/pallas_call | solution.py:584
  266.8 3.2 multiply_reduce_fusion
  270.8 3.7 fusion.37
  292.9 3.0 collective-permute-done.14
  296.0 6.2 %collective-permute-start.16 = (bf16[512,1024]{1,0:T(8,128)(2,1)}, bf16[512,1024]{1,0:T(8,128)(2,1)}, u32[]{:S(2)}, u32[]{:S(2)}) collective-permute-start(bf16[512,1024]{1,0:T(8,128)(2,1)} %add_convert_fusion.1), channel_id=1, source_target_pairs={{0,1},{1,0},{2,3},{3,2},{4,5},{5,4},{6,7},{7,6},{8,9},{9,8},{10,11... | collective-permute-start | bytes 3145736 | tf_op jit(solution)/shard_map/ppermute | solution.py:628
  304.3 37.3 %attention_backward.1 = (bf16[2048,768]{1,0:T(8,128)(2,1)}, bf16[4,2048,2048]{2,1,0:T(8,128)(2,1)}) custom-call(s32[1,4]{1,0:T(1,128)} %len_ref.9, bf16[2048,768]{1,0:T(8,128)(2,1)} %convolution_convert_fusion.q_ref.k_ref.v_ref, bf16[2048,768]{1,0:T(8,128)(2,1)} %convolution_convert_fusion.q_ref.k_ref.v_ref, ...), custom_call_target="tpu_custom_call" | custom-call | flops 8589934592 | bytes 157286400 | tf_op jit(solution)/shard_map/attention_backward/pallas_call | solution.py:366
  343.9 3.8 constant_dynamic-slice_fusion.10
  347.7 5.7 %convolution_convert_fusion.2 = bf16[1024,768]{1,0:T(8,128)(2,1)S(1)} fusion(bf16[2048,1024]{1,0:T(8,128)(2,1)} %all-gather.5.cloned.1.call-done, bf16[2048,768]{1,0:T(8,128)(2,1)S(1)} %copy-done.9), kind=kOutput, calls=%fused_computation.34 | convolution fusion | flops 3222011904 | bytes 8912896 | tf_op jit(solution)/shard_map/dot_general | solution.py:601
  363.0 49.9 %table_grads.1 = f32[32,128]{1,0:T(8,128)} custom-call(s32[1,4]{1,0:T(1,128)} %len_ref.9, bf16[4,2048,2048]{2,1,0:T(8,128)(2,1)} %get-tuple-element.151.ds_ref, s16[2048,2048]{1,0:T(8,128)(2,1)} %get-tuple-element.152.code_ref), custom_call_target="tpu_custom_call" | custom-call | flops 8589934592 | bytes 157286400 | tf_op jit(solution)/shard_map/table_grads/pallas_call | solution.py:478
  415.5 36.9 %collective-permute-done.23 = bf16[128,2304]{1,0:T(8,128)(2,1)} collective-permute-done((bf16[128,2304]{1,0:T(8,128)(2,1)S(1)}, bf16[128,2304]{1,0:T(8,128)(2,1)}, u32[]{:S(2)}, u32[]{:S(2)}) %collective-permute-start.23) | collective-permute-done | bytes 589856 | tf_op jit(solution)/shard_map/ppermute | solution.py:624
  453.5 4.5 collective-permute-start.24
  460.1 7.3 %fusion.14 = (f32[512]{0:T(512)S(1)}, f32[512,1024]{1,0:T(8,128)S(1)}) fusion(bf16[512,1024]{1,0:T(8,128)(2,1)S(1)} %copy-done.2, f32[1024]{0:T(1024)} %copy-done.27, bf16[1024,3072]{1,0:T(8,128)(2,1)} %all-gather.11.cloned.1.call-done, bf16[512,768]{1,0:T(8,128)(2,1)} %collective-permute-done.22, bf16[512,768]{1,0:T(8,128)(2,1)} %collective-permute-done.21, ...), kind=kOutput, calls=%fused_computation.21 | convolution fusion | flops 3235905024 | bytes 12589056 | tf_op jit(solution)/shard_map/dot_general | solution.py:607
  (245 shorter events, 95.6 us)
Async XLA Ops:
  7.2 89.6 %all-gather.5.cloned.1.call-start = ((), (), s32[]{:S(2)}) async-start(), calls=%async_computation.2 | async-start | bytes 5242880 | tf_op jit(solution)/shard_map/all_gather | solution.py:669
  13.2 175.7 %all-gather.7.cloned.1.call-start = ((), (), s32[]{:S(2)}) async-start(), calls=%async_computation.3 | async-start | bytes 2359296 | tf_op jit(solution)/shard_map/all_gather | solution.py:683
  13.3 7.6 %collective-permute-start.10 = (bf16[128,256]{0,1:T(8,128)(2,1)S(1)}, bf16[128,256]{0,1:T(8,128)(2,1)S(1)}, u32[]{:S(2)}, u32[]{:S(2)}) collective-permute-start(bf16[128,256]{0,1:T(8,128)(2,1)S(1)} %dynamic-slice_bitcast_fusion), channel_id=1, source_target_pairs={{0,3},{1,0},{2,1},{3,2},{4,7},{5,4},{6,5},{7,6},{8,11},{9,8},{10,9... | collective-permute-start | bytes 196616 | tf_op jit(solution)/shard_map/ppermute | solution.py:624
  18.4 6.5 %collective-permute-start.9 = (bf16[128,256]{0,1:T(8,128)(2,1)S(1)}, bf16[128,256]{0,1:T(8,128)(2,1)S(1)}, u32[]{:S(2)}, u32[]{:S(2)}) collective-permute-start(bf16[128,256]{0,1:T(8,128)(2,1)S(1)} %dynamic-slice_bitcast_fusion), channel_id=1, source_target_pairs={{0,2},{1,3},{2,0},{3,1},{4,6},{5,7},{6,4},{7,5},{8,10},{9,11},{10,... | collective-permute-start | bytes 196616 | tf_op jit(solution)/shard_map/ppermute | solution.py:624
  25.6 201.3 %all-gather.9.cloned.1.call-start = ((), (), s32[]{:S(2)}) async-start(), calls=%async_computation.4 | async-start | bytes 5308416 | tf_op jit(solution)/shard_map/all_gather | solution.py:701
  96.8 30.1 %collective-permute-start = (bf16[128,2304]{1,0:T(8,128)(2,1)S(1)}, bf16[128,2304]{1,0:T(8,128)(2,1)S(1)}, u32[]{:S(2)}, u32[]{:S(2)}) collective-permute-start(bf16[128,2304]{1,0:T(8,128)(2,1)S(1)} %fusion.24), channel_id=1, source_target_pairs={{0,2},{1,3},{2,0},{3,1},{4,6},{5,7},{6,4},{7,5},{8,10},{9,11},{10,... | collective-permute-start | bytes 1769480 | tf_op jit(solution)/shard_map/ppermute | solution.py:624
  127.8 233.7 %reduce-scatter.3.cloned.1.call-start = ((), (), s32[]{:S(2)}) async-start(), calls=%async_computation.5 | async-start | bytes 10616832 | tf_op jit(solution)/shard_map/reduce_scatter | solution.py:728
  127.8 34.5 %collective-permute-start.1 = (bf16[512,1024]{1,0:T(8,128)(2,1)S(1)}, bf16[512,1024]{1,0:T(8,128)(2,1)}, u32[]{:S(2)}, u32[]{:S(2)}) collective-permute-start(bf16[512,1024]{1,0:T(8,128)(2,1)S(1)} %copy-done.14), channel_id=1, source_target_pairs={{0,1},{1,0},{2,3},{3,2},{4,5},{5,4},{6,7},{7,6},{8,9},{9,8},{10,11... | collective-permute-start | bytes 3145736 | tf_op jit(solution)/shard_map/ppermute | solution.py:628
  129.1 28.9 %collective-permute-start.4 = (bf16[512,128]{1,0:T(8,128)(2,1)S(1)}, bf16[512,128]{1,0:T(8,128)(2,1)S(1)}, u32[]{:S(2)}, u32[]{:S(2)}) collective-permute-start(bf16[512,128]{1,0:T(8,128)(2,1)S(1)} %get-tuple-element.215), channel_id=1, source_target_pairs={{0,3},{1,0},{2,1},{3,2},{4,7},{5,4},{6,5},{7,6},{8,11},{9,8},{10,9... | collective-permute-start | bytes 393224 | tf_op jit(solution)/shard_map/ppermute | solution.py:624
  132.4 25.6 %collective-permute-start.3 = (bf16[512,128]{1,0:T(8,128)(2,1)S(1)}, bf16[512,128]{1,0:T(8,128)(2,1)S(1)}, u32[]{:S(2)}, u32[]{:S(2)}) collective-permute-start(bf16[512,128]{1,0:T(8,128)(2,1)S(1)} %get-tuple-element.216), channel_id=1, source_target_pairs={{0,2},{1,3},{2,0},{3,1},{4,6},{5,7},{6,4},{7,5},{8,10},{9,11},{10,... | collective-permute-start | bytes 393224 | tf_op jit(solution)/shard_map/ppermute | solution.py:624
  132.6 29.7 %collective-permute-start.2 = (bf16[512,128]{1,0:T(8,128)(2,1)S(1)}, bf16[512,128]{1,0:T(8,128)(2,1)S(1)}, u32[]{:S(2)}, u32[]{:S(2)}) collective-permute-start(bf16[512,128]{1,0:T(8,128)(2,1)S(1)} %get-tuple-element.217), channel_id=1, source_target_pairs={{0,1},{1,2},{2,3},{3,0},{4,5},{5,6},{6,7},{7,4},{8,9},{9,10},{10,1... | collective-permute-start | bytes 393224 | tf_op jit(solution)/shard_map/ppermute | solution.py:624
  164.8 17.8 %collective-permute-start.5 = (bf16[512,128]{1,0:T(8,128)(2,1)S(1)}, bf16[512,128]{1,0:T(8,128)(2,1)S(1)}, u32[]{:S(2)}, u32[]{:S(2)}) collective-permute-start(bf16[512,128]{1,0:T(8,128)(2,1)S(1)} %get-tuple-element.213), channel_id=1, source_target_pairs={{0,1},{1,2},{2,3},{3,0},{4,5},{5,6},{6,7},{7,4},{8,9},{9,10},{10,1... | collective-permute-start | bytes 393224 | tf_op jit(solution)/shard_map/ppermute | solution.py:624
  174.3 13.9 %collective-permute-start.7 = (bf16[512,128]{1,0:T(8,128)(2,1)S(1)}, bf16[512,128]{1,0:T(8,128)(2,1)S(1)}, u32[]{:S(2)}, u32[]{:S(2)}) collective-permute-start(bf16[512,128]{1,0:T(8,128)(2,1)S(1)} %get-tuple-element.211), channel_id=1, source_target_pairs={{0,3},{1,0},{2,1},{3,2},{4,7},{5,4},{6,5},{7,6},{8,11},{9,8},{10,9... | collective-permute-start | bytes 393224 | tf_op jit(solution)/shard_map/ppermute | solution.py:624
  178.1 8.7 %collective-permute-start.6 = (bf16[512,128]{1,0:T(8,128)(2,1)S(1)}, bf16[512,128]{1,0:T(8,128)(2,1)S(1)}, u32[]{:S(2)}, u32[]{:S(2)}) collective-permute-start(bf16[512,128]{1,0:T(8,128)(2,1)S(1)} %get-tuple-element.212), channel_id=1, source_target_pairs={{0,2},{1,3},{2,0},{3,1},{4,6},{5,7},{6,4},{7,5},{8,10},{9,11},{10,... | collective-permute-start | bytes 393224 | tf_op jit(solution)/shard_map/ppermute | solution.py:624
  192.4 24.6 %collective-permute-start.11 = (bf16[512,1024]{1,0:T(8,128)(2,1)S(1)}, bf16[512,1024]{1,0:T(8,128)(2,1)S(1)}, u32[]{:S(2)}, u32[]{:S(2)}) collective-permute-start(bf16[512,1024]{1,0:T(8,128)(2,1)S(1)} %multiply_convert_fusion.x_ref.refs_0_), channel_id=1, source_target_pairs={{0,1},{1,0},{2,3},{3,2},{4,5},{5,4},{6,7},{7,6},{8,9},{9,8},{10,11... | collective-permute-start | bytes 3145736 | tf_op jit(solution)/shard_map/ppermute | solution.py:628
  239.1 25.6 %collective-permute-start.12 = (bf16[512,1024]{1,0:T(8,128)(2,1)}, bf16[512,1024]{1,0:T(8,128)(2,1)}, u32[]{:S(2)}, u32[]{:S(2)}) collective-permute-start(bf16[512,1024]{1,0:T(8,128)(2,1)} %add_convert_fusion.2), channel_id=1, source_target_pairs={{0,1},{1,0},{2,3},{3,2},{4,5},{5,4},{6,7},{7,6},{8,9},{9,8},{10,11... | collective-permute-start | bytes 3145736 | tf_op jit(solution)/shard_map/ppermute | solution.py:628
  264.7 195.4 %all-gather.11.cloned.1.call-start = ((), (), s32[]{:S(2)}) async-start(), calls=%async_computation.6 | async-start | bytes 7077888 | tf_op jit(solution)/shard_map/all_gather | solution.py:764
  276.0 20.0 %collective-permute-start.15 = (bf16[512,256]{1,0:T(8,128)(2,1)S(1)}, bf16[512,256]{1,0:T(8,128)(2,1)S(1)}, u32[]{:S(2)}, u32[]{:S(2)}) collective-permute-start(bf16[512,256]{1,0:T(8,128)(2,1)S(1)} %get-tuple-element.207), channel_id=1, source_target_pairs={{0,1},{1,2},{2,3},{3,0},{4,5},{5,6},{6,7},{7,4},{8,9},{9,10},{10,1... | collective-permute-start | bytes 786440 | tf_op jit(solution)/shard_map/ppermute | solution.py:624
  277.7 18.3 %collective-permute-start.14 = (bf16[512,256]{1,0:T(8,128)(2,1)S(1)}, bf16[512,256]{1,0:T(8,128)(2,1)S(1)}, u32[]{:S(2)}, u32[]{:S(2)}) collective-permute-start(bf16[512,256]{1,0:T(8,128)(2,1)S(1)} %get-tuple-element.208), channel_id=1, source_target_pairs={{0,2},{1,3},{2,0},{3,1},{4,6},{5,7},{6,4},{7,5},{8,10},{9,11},{10,... | collective-permute-start | bytes 786440 | tf_op jit(solution)/shard_map/ppermute | solution.py:624
  277.7 15.2 %collective-permute-start.13 = (bf16[512,256]{1,0:T(8,128)(2,1)S(1)}, bf16[512,256]{1,0:T(8,128)(2,1)S(1)}, u32[]{:S(2)}, u32[]{:S(2)}) collective-permute-start(bf16[512,256]{1,0:T(8,128)(2,1)S(1)} %get-tuple-element.209), channel_id=1, source_target_pairs={{0,3},{1,0},{2,1},{3,2},{4,7},{5,4},{6,5},{7,6},{8,11},{9,8},{10,9... | collective-permute-start | bytes 786440 | tf_op jit(solution)/shard_map/ppermute | solution.py:624
  296.0 45.7 %collective-permute-start.16 = (bf16[512,1024]{1,0:T(8,128)(2,1)}, bf16[512,1024]{1,0:T(8,128)(2,1)}, u32[]{:S(2)}, u32[]{:S(2)}) collective-permute-start(bf16[512,1024]{1,0:T(8,128)(2,1)} %add_convert_fusion.1), channel_id=1, source_target_pairs={{0,1},{1,0},{2,3},{3,2},{4,5},{5,4},{6,7},{7,6},{8,9},{9,8},{10,11... | collective-permute-start | bytes 3145736 | tf_op jit(solution)/shard_map/ppermute | solution.py:628
  302.2 39.5 %collective-permute-start.19 = (bf16[128,768]{1,0:T(8,128)(2,1)}, bf16[128,768]{1,0:T(8,128)(2,1)S(1)}, u32[]{:S(2)}, u32[]{:S(2)}) collective-permute-start(bf16[128,768]{1,0:T(8,128)(2,1)} %constant_dynamic-slice_fusion.14), channel_id=1, source_target_pairs={{0,3},{1,0},{2,1},{3,2},{4,7},{5,4},{6,5},{7,6},{8,11},{9,8},{10,9... | collective-permute-start | bytes 589832 | tf_op jit(solution)/shard_map/ppermute | solution.py:624
  302.6 39.0 %collective-permute-start.18 = (bf16[128,768]{1,0:T(8,128)(2,1)}, bf16[128,768]{1,0:T(8,128)(2,1)S(1)}, u32[]{:S(2)}, u32[]{:S(2)}) collective-permute-start(bf16[128,768]{1,0:T(8,128)(2,1)} %constant_dynamic-slice_fusion.14), channel_id=1, source_target_pairs={{0,2},{1,3},{2,0},{3,1},{4,6},{5,7},{6,4},{7,5},{8,10},{9,11},{10,... | collective-permute-start | bytes 589832 | tf_op jit(solution)/shard_map/ppermute | solution.py:624
  303.7 37.9 %collective-permute-start.17 = (bf16[128,768]{1,0:T(8,128)(2,1)}, bf16[128,768]{1,0:T(8,128)(2,1)S(1)}, u32[]{:S(2)}, u32[]{:S(2)}) collective-permute-start(bf16[128,768]{1,0:T(8,128)(2,1)} %constant_dynamic-slice_fusion.14), channel_id=1, source_target_pairs={{0,1},{1,2},{2,3},{3,0},{4,5},{5,6},{6,7},{7,4},{8,9},{9,10},{10,1... | collective-permute-start | bytes 589832 | tf_op jit(solution)/shard_map/ppermute | solution.py:624
  343.6 129.5 %reduce-scatter.5.cloned.1.call-start = ((), (), s32[]{:S(2)}) async-start(), calls=%async_computation.7 | async-start | bytes 4128768 | tf_op jit(solution)/shard_map/reduce_scatter | solution.py:771
  355.6 59.9 %collective-permute-start.20 = (bf16[512,768]{1,0:T(8,128)(2,1)}, bf16[512,768]{1,0:T(8,128)(2,1)}, u32[]{:S(2)}, u32[]{:S(2)}) collective-permute-start(bf16[512,768]{1,0:T(8,128)(2,1)} %get-tuple-element.154), channel_id=1, source_target_pairs={{0,1},{1,2},{2,3},{3,0},{4,5},{5,6},{6,7},{7,4},{8,9},{9,10},{10,1... | collective-permute-start | bytes 2359304 | tf_op jit(solution)/shard_map/ppermute | solution.py:624
  357.4 58.0 %collective-permute-start.21 = (bf16[512,768]{1,0:T(8,128)(2,1)S(1)}, bf16[512,768]{1,0:T(8,128)(2,1)}, u32[]{:S(2)}, u32[]{:S(2)}) collective-permute-start(bf16[512,768]{1,0:T(8,128)(2,1)S(1)} %copy-done.18), channel_id=1, source_target_pairs={{0,2},{1,3},{2,0},{3,1},{4,6},{5,7},{6,4},{7,5},{8,10},{9,11},{10,... | collective-permute-start | bytes 2359304 | tf_op jit(solution)/shard_map/ppermute | solution.py:624
  359.5 56.0 %collective-permute-start.22 = (bf16[512,768]{1,0:T(8,128)(2,1)S(1)}, bf16[512,768]{1,0:T(8,128)(2,1)}, u32[]{:S(2)}, u32[]{:S(2)}) collective-permute-start(bf16[512,768]{1,0:T(8,128)(2,1)S(1)} %copy-done.17), channel_id=1, source_target_pairs={{0,3},{1,0},{2,1},{3,2},{4,7},{5,4},{6,5},{7,6},{8,11},{9,8},{10,9... | collective-permute-start | bytes 2359304 | tf_op jit(solution)/shard_map/ppermute | solution.py:624
  362.6 89.7 %collective-permute-start.23 = (bf16[128,2304]{1,0:T(8,128)(2,1)S(1)}, bf16[128,2304]{1,0:T(8,128)(2,1)}, u32[]{:S(2)}, u32[]{:S(2)}) collective-permute-start(bf16[128,2304]{1,0:T(8,128)(2,1)S(1)} %slice.138), channel_id=1, source_target_pairs={{0,2},{1,3},{2,0},{3,1},{4,6},{5,7},{6,4},{7,5},{8,10},{9,11},{10,... | collective-permute-start | bytes 1769480 | tf_op jit(solution)/shard_map/ppermute | solution.py:624
  453.5 19.0 %collective-permute-start.24 = (f32[4,12,4]{1,0,2:T(4,128)}, f32[4,12,4]{1,0,2:T(4,128)}, u32[]{:S(2)}, u32[]{:S(2)}) collective-permute-start(f32[4,12,4]{1,0,2:T(4,128)} %fusion.26), channel_id=1, source_target_pairs={{0,16},{4,20},{8,24},{12,28},{16,0},{20,4},{24,8},{28,12},{1,17},{... | collective-permute-start | bytes 2312 | tf_op jit(solution)/shard_map/ppermute | solution.py:786
  476.2 11.1 %collective-permute-start.31 = (f32[2,12,4]{1,0,2:T(2,128)S(1)}, f32[2,12,4]{1,0,2:T(2,128)S(1)}, u32[]{:S(2)}, u32[]{:S(2)}) collective-permute-start(f32[2,12,4]{1,0,2:T(2,128)S(1)} %constant_dynamic-slice_fusion.3), channel_id=1, source_target_pairs={{0,8},{4,12},{8,0},{12,4},{16,24},{20,28},{24,16},{28,20},{1,9},{5... | collective-permute-start | bytes 1160 | tf_op jit(solution)/shard_map/ppermute | solution.py:786
  477.0 13.0 %collective-permute-start.28 = (bf16[128,256]{1,0:T(8,128)(2,1)S(1)}, bf16[128,256]{1,0:T(8,128)(2,1)S(1)}, u32[]{:S(2)}, u32[]{:S(2)}) collective-permute-start(bf16[128,256]{1,0:T(8,128)(2,1)S(1)} %get-tuple-element.219), channel_id=1, source_target_pairs={{0,3},{1,0},{2,1},{3,2},{4,7},{5,4},{6,5},{7,6},{8,11},{9,8},{10,9... | collective-permute-start | bytes 196616 | tf_op jit(solution)/shard_map/ppermute | solution.py:624
  (51 other events, 563.2 us)
Sparse Core Ops, SparseCore 0:
  13.3 83.4 all-gather.4
  99.3 26.8 all-gather.6
  128.6 38.8 all-gather.8
  264.8 78.3 reduce-scatter.2
  344.9 46.9 all-gather.10
  395.2 48.7 reduce-scatter.4
